TPU v7x, 32 devices: a whole 2x2x4 slice. The times are simulated.
32 devices in a mesh: seq: 8 (over y, x, core), head: 4 (over z).
Axes of the slice: x: 2, y: 2, z: 4, core: 2. Of those that a mesh axis runs over, the one named last changes fastest.
Arguments:
- queries: bfloat16 [8192, 8192], P('seq', 'head'), may hold values from -6 to 6
- key_rows: bfloat16 [8192, 8192], P('seq', 'head'), may hold values from -6 to 6
- value_rows: bfloat16 [8192, 8192], P('seq', 'head')
- log_decay: float32 [64, 8192], P('head', 'seq')
- doc_start: int32 [8192], P('seq'), may hold values from 0 to 1, as said below
- gate_input: bfloat16 [8192, 8192], P('seq', 'head'), may hold values from -6 to 6
- norm_gain: float32 [8192], P('head'), may hold values from 0.1 to 1.9
- out_grad: bfloat16 [8192, 8192], P('seq', 'head'), may hold values from -6 to 6
Outputs:
- gated: bfloat16 [8192, 8192], P('seq', 'head')
- gate_grad: bfloat16 [8192, 8192], P('seq', 'head')
- query_grad: bfloat16 [8192, 8192], P('seq', 'head')
- key_grad: bfloat16 [8192, 8192], P('seq', 'head')
- value_grad: bfloat16 [8192, 8192], P('seq', 'head')
Inputs may be any that keep to these rules, and one draw needn't show every extreme that they name: `doc_start`: only the first 512 and the last 512 tokens of the sequence can begin a document, and each of these two ranges holds at least one start; one document runs over all devices but the first and the last.
All inputs are finite; a program needn't handle non-finite values.
Results may differ from a plain program's by a relative error of at most 0.0062.
Values sent between devices are 32-bit elements; how exact they have to be, the bound alone decides.
No kernel may reach another device: no remote copies, remote signals or barrier semaphores. Data moves between devices by JAX's collectives and lax.ppermute only.
A program may use at most 128 MiB of HBM per device.

v0:
```python
import jax
import jax.numpy as jnp
from jax import lax
from jax.sharding import PartitionSpec as P

HEAD_TOTAL = 64
HD = 128
BLOCK = 512


epsilon = 1e-06


def passed_along(block, axis, distance):
    devices = range(lax.axis_size(axis))
    route = [(i - distance, i) for i in devices if i - distance in devices]
    return lax.ppermute(block, axis, route)


def block_terms(log_rates, start_flags):
    cumulative = jnp.cumsum(log_rates, axis=-1)
    doc_count = jnp.cumsum(start_flags, axis=-1, dtype=jnp.int32)
    length = start_flags.shape[-1]
    position = jnp.arange(length, dtype=jnp.int32)
    allowed = (doc_count[:, None] == doc_count[None, :]) & (position[:, None] >= position[None, :])
    difference = jnp.where(allowed[None], cumulative[:, :, None] - cumulative[:, None, :], 0.0)
    weight = jnp.where(allowed[None], jnp.exp(difference), 0.0)
    entering = jnp.where((doc_count == 0)[None], jnp.exp(cumulative), 0.0)
    last_doc = doc_count[-1]
    leaving = jnp.where(
        (doc_count == last_doc)[None], jnp.exp(cumulative[:, -1:] - cumulative), 0.0
    )
    passing = jnp.where(last_doc == 0, jnp.exp(cumulative[:, -1]), 0.0)
    return (weight, entering, leaving, passing)


def forward_prefix(total_pass, dev_state):

    def forward_advance(step, carried):
        received, inclusive = carried
        arrived = passed_along(inclusive, "seq", 1)
        return (arrived, total_pass[:, None, None] * arrived + dev_state)

    arrived, _ = lax.fori_loop(
        0, lax.axis_size("seq") - 1, forward_advance, (jnp.zeros_like(dev_state), dev_state)
    )
    return arrived


def backward_prefix(total_pass, dev_back):

    def backward_advance(step, carried):
        received, inclusive = carried
        arrived = passed_along(inclusive, "seq", -1)
        return (arrived, dev_back + total_pass[:, None, None] * arrived)

    arrived, _ = lax.fori_loop(
        0, lax.axis_size("seq") - 1, backward_advance, (jnp.zeros_like(dev_back), dev_back)
    )
    return arrived


def body(queries, key_rows, value_rows, log_decay, doc_start, gate_input, norm_gain, out_grad):
    row_count, width_dev = queries.shape
    head_count = width_dev // HD
    width = HEAD_TOTAL * HD
    blocks_dev = row_count // BLOCK
    query_block = queries.reshape(blocks_dev, BLOCK, head_count, HD)
    key_block = key_rows.reshape(blocks_dev, BLOCK, head_count, HD)
    value_block = value_rows.reshape(blocks_dev, BLOCK, head_count, HD)
    rate_block = log_decay.reshape(head_count, blocks_dev, BLOCK).transpose(1, 0, 2)
    start_block = doc_start.reshape(blocks_dev, BLOCK)
    weight, entering, leaving, passing = jax.vmap(block_terms)(rate_block, start_block)
    enter_rows = jnp.swapaxes(entering, 1, 2)[..., None]
    leave_rows = jnp.swapaxes(leaving, 1, 2)[..., None]
    scores = jnp.einsum(
        "nthd,nshd->nhts", query_block, key_block, preferred_element_type=jnp.float32
    )
    weights_bf = (scores * weight).astype(jnp.bfloat16)
    inside = jnp.einsum(
        "nhts,nshe->nthe", weights_bf, value_block, preferred_element_type=jnp.float32
    )
    keyed = (key_block * leave_rows).astype(jnp.bfloat16)
    local = jnp.einsum("nshd,nshe->nhde", keyed, value_block, preferred_element_type=jnp.float32)
    total_pass = jnp.ones((head_count,), jnp.float32)
    dev_state = jnp.zeros((head_count, HD, HD), jnp.float32)
    for index in range(blocks_dev):
        dev_state = passing[index][:, None, None] * dev_state + local[index]
        total_pass = total_pass * passing[index]
    incoming = forward_prefix(total_pass, dev_state)
    carried = incoming
    held_list = []
    for index in range(blocks_dev):
        held_list.append(carried.astype(jnp.bfloat16))
        carried = passing[index][:, None, None] * carried + local[index]
    held = jnp.stack(held_list)
    outside = (
        jnp.einsum("nthd,nhde->nthe", query_block, held, preferred_element_type=jnp.float32)
        * enter_rows
    )
    attn = (inside + outside).reshape(row_count, width_dev)
    sig = jax.nn.sigmoid(gate_input.astype(jnp.float32))
    grad_f = out_grad.astype(jnp.float32)
    gnorm = grad_f * sig
    squares, inner = lax.psum(
        (jnp.sum(attn * attn, axis=1), jnp.sum(gnorm * norm_gain[None, :] * attn, axis=1)), "head"
    )
    inverse = lax.rsqrt(squares / width + epsilon)
    normed = attn * inverse[:, None] * norm_gain[None, :]
    gated = (normed * sig).astype(jnp.bfloat16)
    gate_grad = (grad_f * normed * sig * (1.0 - sig)).astype(jnp.bfloat16)
    cube = inverse * inverse * inverse
    attn_grad = (
        inverse[:, None] * norm_gain[None, :] * gnorm
        - attn * cube[:, None] * inner[:, None] / width
    ).astype(jnp.bfloat16)
    agrad_block = attn_grad.reshape(blocks_dev, BLOCK, head_count, HD)
    dscore = (
        jnp.einsum("nthe,nshe->nhts", agrad_block, value_block, preferred_element_type=jnp.float32)
        * weight
    ).astype(jnp.bfloat16)
    qkeyed = (query_block * enter_rows).astype(jnp.bfloat16)
    back_local = jnp.einsum(
        "nthd,nthe->nhde", qkeyed, agrad_block, preferred_element_type=jnp.float32
    )
    dev_back = jnp.zeros((head_count, HD, HD), jnp.float32)
    for index in reversed(range(blocks_dev)):
        dev_back = back_local[index] + passing[index][:, None, None] * dev_back
    outgoing = backward_prefix(total_pass, dev_back)
    behind = outgoing
    back_list = [None] * blocks_dev
    for index in reversed(range(blocks_dev)):
        back_list[index] = behind.astype(jnp.bfloat16)
        behind = back_local[index] + passing[index][:, None, None] * behind
    back_held = jnp.stack(back_list)
    qgrad = jnp.einsum("nhts,nshd->nthd", dscore, key_block, preferred_element_type=jnp.float32)
    qgrad = qgrad + enter_rows * jnp.einsum(
        "nthe,nhde->nthd", agrad_block, held, preferred_element_type=jnp.float32
    )
    kgrad = jnp.einsum("nhts,nthd->nshd", dscore, query_block, preferred_element_type=jnp.float32)
    kgrad = kgrad + leave_rows * jnp.einsum(
        "nshe,nhde->nshd", value_block, back_held, preferred_element_type=jnp.float32
    )
    vgrad = jnp.einsum(
        "nhts,nthe->nshe", weights_bf, agrad_block, preferred_element_type=jnp.float32
    )
    vgrad = vgrad + leave_rows * jnp.einsum(
        "nshd,nhde->nshe", key_block, back_held, preferred_element_type=jnp.float32
    )
    query_grad = qgrad.reshape(row_count, width_dev).astype(jnp.bfloat16)
    key_grad = kgrad.reshape(row_count, width_dev).astype(jnp.bfloat16)
    value_grad = vgrad.reshape(row_count, width_dev).astype(jnp.bfloat16)
    return (gated, gate_grad, query_grad, key_grad, value_grad)


def solution(mesh):
    in_specs = (
        P("seq", "head"),
        P("seq", "head"),
        P("seq", "head"),
        P("head", "seq"),
        P("seq"),
        P("seq", "head"),
        P("head"),
        P("seq", "head"),
    )
    out_specs = (
        P("seq", "head"),
        P("seq", "head"),
        P("seq", "head"),
        P("seq", "head"),
        P("seq", "head"),
    )
    return jax.shard_map(body, mesh=mesh, in_specs=in_specs, out_specs=out_specs, check_vma=False)
```

profile of v0, /device:TPU:3, one launch (start us, length us, event | category | flops | bytes accessed | tf_op | source)
XLA Modules:
  0.0 507.9 jit_solution(6392769854963522176)
XLA Ops:
  37.0 124.2 %while.24 = (s32[]{:T(128)}, f32[16,128,128]{2,1,0:T(8,128)}, f32[16,128,128]{2,1,0:T(8,128)S(1)}, f32[16]{0:T(128)S(1)}, f32[16,128,128]{2,1,0:T(8,128)S(1)}, /*index=5*/s32[]{:T(128)}) while((s32[]{:T(128)}, f32[16,128,128]{2,1,0:T(8,128)}, f32[16,128,128]{2,1,0:T(8,128)S(1)}, f32[16]{0:T(128)S(1)}, f32[16,128,128]{2,1,0:T(8,128)S(1)}, ...), condition=%wide.region_5.6_spmd, body=%wide.region_4.5_spmd.sunk | while | flops 524290 | bytes 11534537 | solution.py:44
  40.7 11.7 %collective-permute-done = f32[16,128,128]{2,1,0:T(8,128)S(1)} collective-permute-done((f32[16,128,128]{2,1,0:T(8,128)S(1)}, f32[16,128,128]{2,1,0:T(8,128)S(1)}, u32[]{:S(2)}, u32[]{:S(2)}) %collective-permute-start) | collective-permute-done | bytes 1048608 | tf_op jit(solution)/shard_map/while/body/eval_jaxpr/ppermute | solution.py:17
  58.7 11.7 %collective-permute-done = f32[16,128,128]{2,1,0:T(8,128)S(1)} collective-permute-done((f32[16,128,128]{2,1,0:T(8,128)S(1)}, f32[16,128,128]{2,1,0:T(8,128)S(1)}, u32[]{:S(2)}, u32[]{:S(2)}) %collective-permute-start) | collective-permute-done | bytes 1048608 | tf_op jit(solution)/shard_map/while/body/eval_jaxpr/ppermute | solution.py:17
  76.6 11.7 %collective-permute-done = f32[16,128,128]{2,1,0:T(8,128)S(1)} collective-permute-done((f32[16,128,128]{2,1,0:T(8,128)S(1)}, f32[16,128,128]{2,1,0:T(8,128)S(1)}, u32[]{:S(2)}, u32[]{:S(2)}) %collective-permute-start) | collective-permute-done | bytes 1048608 | tf_op jit(solution)/shard_map/while/body/eval_jaxpr/ppermute | solution.py:17
  94.6 11.7 %collective-permute-done = f32[16,128,128]{2,1,0:T(8,128)S(1)} collective-permute-done((f32[16,128,128]{2,1,0:T(8,128)S(1)}, f32[16,128,128]{2,1,0:T(8,128)S(1)}, u32[]{:S(2)}, u32[]{:S(2)}) %collective-permute-start) | collective-permute-done | bytes 1048608 | tf_op jit(solution)/shard_map/while/body/eval_jaxpr/ppermute | solution.py:17
  112.6 11.7 %collective-permute-done = f32[16,128,128]{2,1,0:T(8,128)S(1)} collective-permute-done((f32[16,128,128]{2,1,0:T(8,128)S(1)}, f32[16,128,128]{2,1,0:T(8,128)S(1)}, u32[]{:S(2)}, u32[]{:S(2)}) %collective-permute-start) | collective-permute-done | bytes 1048608 | tf_op jit(solution)/shard_map/while/body/eval_jaxpr/ppermute | solution.py:17
  130.6 11.7 %collective-permute-done = f32[16,128,128]{2,1,0:T(8,128)S(1)} collective-permute-done((f32[16,128,128]{2,1,0:T(8,128)S(1)}, f32[16,128,128]{2,1,0:T(8,128)S(1)}, u32[]{:S(2)}, u32[]{:S(2)}) %collective-permute-start) | collective-permute-done | bytes 1048608 | tf_op jit(solution)/shard_map/while/body/eval_jaxpr/ppermute | solution.py:17
  148.5 11.7 %collective-permute-done = f32[16,128,128]{2,1,0:T(8,128)S(1)} collective-permute-done((f32[16,128,128]{2,1,0:T(8,128)S(1)}, f32[16,128,128]{2,1,0:T(8,128)S(1)}, u32[]{:S(2)}, u32[]{:S(2)}) %collective-permute-start) | collective-permute-done | bytes 1048608 | tf_op jit(solution)/shard_map/while/body/eval_jaxpr/ppermute | solution.py:17
  163.4 19.6 %multiply_convert_fusion.1 = bf16[2,16,512,512]{3,2,1,0:T(8,128)(2,1)} fusion(bf16[2,512,16,128]{1,3,2,0:T(8,128)(2,1)} %copy.92, f32[2,16,512]{2,1,0:T(8,128)S(1)} %copy_bitcast_fusion.3, pred[2,512,512]{2,1,0:T(8,128)(4,1)} %compare_and_fusion, bf16[2,512,16,128]{3,2,1,0:T(8,128)(2,1)} %bitcast.181), kind=kOutput, calls=%fused_computation.3 | convolution fusion | flops 2189426688 | bytes 25755648 | tf_op jit(solution)/shard_map/nthd,nshd->nhts/dot_general | solution.py:76
  183.0 12.7 %fusion.21 = f32[2,16,512,128]{2,3,1,0:T(8,128)} fusion(bf16[2,16,512,512]{3,2,1,0:T(8,128)(2,1)} %multiply_convert_fusion.1, bf16[2,512,16,128]{3,2,1,0:T(8,128)(2,1)} %bitcast.177), kind=kOutput, calls=%fused_computation.43 | convolution fusion | flops 2147483648 | bytes 29360128 | tf_op jit(solution)/shard_map/nhts,nshe->nthe/dot_general | solution.py:80
  233.1 13.1 %fusion.18 = (bf16[128,8,16,128]{3,1,2,0:T(8,128)(2,1)S(1)}, bf16[1024,2048]{1,0:T(8,128)(2,1)}, bf16[1024,2048]{1,0:T(8,128)(2,1)}) fusion(f32[128,8,16,128]{3,2,1,0:T(8,128)} %bitcast.175, bf16[1024,2048]{1,0:T(8,128)(2,1)} %param.19, f32[1024]{0:T(1024)S(1)} %get-tuple-element.80, f32[1024]{0:T(1024)S(1)} %get-tuple-element.90, f32[2048]{0:T(1024)S(1)} %copy-done.14, ...), kind=kLoop, calls=%fused_computation.37 | loop fusion | flops 46137344 | bytes 29380608
  257.1 11.5 %fusion.41 = f32[2,16,128,512]{2,3,1,0:T(8,128)} fusion(bf16[2,512,16,128]{1,3,2,0:T(8,128)(2,1)} %copy.97, bf16[2,16,512,512]{3,2,1,0:T(8,128)(2,1)} %multiply_convert_fusion.1), kind=kOutput, calls=%fused_computation.96 | convolution fusion | flops 2147483648 | bytes 29360128 | tf_op jit(solution)/shard_map/nhts,nthe->nshe/dot_general | solution.py:144
  277.0 132.4 %while.25 = (s32[]{:T(128)}, f32[16,128,128]{2,1,0:T(8,128)}, f32[16,128,128]{2,1,0:T(8,128)}, f32[16]{0:T(128)S(1)}, f32[16,128,128]{2,1,0:T(8,128)S(1)}, /*index=5*/s32[]{:T(128)}) while((s32[]{:T(128)}, f32[16,128,128]{2,1,0:T(8,128)}, f32[16,128,128]{2,1,0:T(8,128)}, f32[16]{0:T(128)S(1)}, f32[16,128,128]{2,1,0:T(8,128)S(1)}, ...), condition=%wide.region_11.12_spmd, body=%wide.region_10.11_spmd.sunk | while | flops 524290 | bytes 11534537 | solution.py:57
  278.9 18.1 %collective-permute-done.1 = f32[16,128,128]{2,1,0:T(8,128)S(1)} collective-permute-done((f32[16,128,128]{2,1,0:T(8,128)}, f32[16,128,128]{2,1,0:T(8,128)S(1)}, u32[]{:S(2)}, u32[]{:S(2)}) %collective-permute-start.1) | collective-permute-done | bytes 1048608 | tf_op jit(solution)/shard_map/while/body/eval_jaxpr/ppermute | solution.py:17
  300.2 15.3 %collective-permute-done.1 = f32[16,128,128]{2,1,0:T(8,128)S(1)} collective-permute-done((f32[16,128,128]{2,1,0:T(8,128)}, f32[16,128,128]{2,1,0:T(8,128)S(1)}, u32[]{:S(2)}, u32[]{:S(2)}) %collective-permute-start.1) | collective-permute-done | bytes 1048608 | tf_op jit(solution)/shard_map/while/body/eval_jaxpr/ppermute | solution.py:17
  318.7 15.3 %collective-permute-done.1 = f32[16,128,128]{2,1,0:T(8,128)S(1)} collective-permute-done((f32[16,128,128]{2,1,0:T(8,128)}, f32[16,128,128]{2,1,0:T(8,128)S(1)}, u32[]{:S(2)}, u32[]{:S(2)}) %collective-permute-start.1) | collective-permute-done | bytes 1048608 | tf_op jit(solution)/shard_map/while/body/eval_jaxpr/ppermute | solution.py:17
  337.2 15.3 %collective-permute-done.1 = f32[16,128,128]{2,1,0:T(8,128)S(1)} collective-permute-done((f32[16,128,128]{2,1,0:T(8,128)}, f32[16,128,128]{2,1,0:T(8,128)S(1)}, u32[]{:S(2)}, u32[]{:S(2)}) %collective-permute-start.1) | collective-permute-done | bytes 1048608 | tf_op jit(solution)/shard_map/while/body/eval_jaxpr/ppermute | solution.py:17
  355.7 15.3 %collective-permute-done.1 = f32[16,128,128]{2,1,0:T(8,128)S(1)} collective-permute-done((f32[16,128,128]{2,1,0:T(8,128)}, f32[16,128,128]{2,1,0:T(8,128)S(1)}, u32[]{:S(2)}, u32[]{:S(2)}) %collective-permute-start.1) | collective-permute-done | bytes 1048608 | tf_op jit(solution)/shard_map/while/body/eval_jaxpr/ppermute | solution.py:17
  374.3 15.3 %collective-permute-done.1 = f32[16,128,128]{2,1,0:T(8,128)S(1)} collective-permute-done((f32[16,128,128]{2,1,0:T(8,128)}, f32[16,128,128]{2,1,0:T(8,128)S(1)}, u32[]{:S(2)}, u32[]{:S(2)}) %collective-permute-start.1) | collective-permute-done | bytes 1048608 | tf_op jit(solution)/shard_map/while/body/eval_jaxpr/ppermute | solution.py:17
  392.8 15.3 %collective-permute-done.1 = f32[16,128,128]{2,1,0:T(8,128)S(1)} collective-permute-done((f32[16,128,128]{2,1,0:T(8,128)}, f32[16,128,128]{2,1,0:T(8,128)S(1)}, u32[]{:S(2)}, u32[]{:S(2)}) %collective-permute-start.1) | collective-permute-done | bytes 1048608 | tf_op jit(solution)/shard_map/while/body/eval_jaxpr/ppermute | solution.py:17
  411.5 14.6 %fusion.10 = bf16[2,512,16,128]{3,1,2,0:T(8,128)(2,1)S(1)} fusion(f32[2,16,128,512]{2,3,1,0:T(8,128)} %fusion.41, f32[2,512,16]{1,2,0:T(8,128)S(1)} %get-tuple-element.88, bf16[2,512,16,128]{3,2,1,0:T(8,128)(2,1)} %bitcast.182, bf16[1,16,128,128]{3,2,1,0:T(8,128)(2,1)S(1)} %get-tuple-element.85, bf16[1,16,128,128]{3,2,1,0:T(8,128)(2,1)S(1)} %get-tuple-element.84), kind=kOutput, calls=%fused_computation.21 | convolution fusion | flops 545259520 | bytes 17891328 | tf_op jit(solution)/shard_map/nshd,nhde->nshe/dot_general | solution.py:147
  430.8 14.0 %multiply_convert_fusion = bf16[2,16,512,512]{3,2,1,0:T(8,128)(2,1)} fusion(bf16[2,512,16,128]{1,3,2,0:T(8,128)(2,1)S(1)} %copy-done, f32[2,16,512]{2,1,0:T(8,128)S(1)} %copy_bitcast_fusion.3, pred[2,512,512]{2,1,0:T(8,128)(4,1)S(1)} %copy-done.13, bf16[2,512,16,128]{3,2,1,0:T(8,128)(2,1)S(1)} %bitcast.178), kind=kOutput, calls=%fused_computation.2 | convolution fusion | flops 2189426688 | bytes 25755648 | tf_op jit(solution)/shard_map/nthe,nshe->nhts/dot_general | solution.py:119
  444.8 11.4 %fusion.40 = f32[2,16,512,128]{3,2,1,0:T(8,128)} fusion(bf16[2,16,512,512]{3,2,1,0:T(8,128)(2,1)} %multiply_convert_fusion, bf16[2,512,16,128]{1,3,2,0:T(8,128)(2,1)} %copy.92), kind=kOutput, calls=%fused_computation.95 | convolution fusion | flops 2147483648 | bytes 29360128 | tf_op jit(solution)/shard_map/nhts,nthd->nshd/dot_general | solution.py:140
  456.2 12.4 %fusion.27 = f32[2,16,512,128]{2,3,1,0:T(8,128)} fusion(bf16[2,16,512,512]{3,2,1,0:T(8,128)(2,1)} %multiply_convert_fusion, bf16[2,512,16,128]{3,2,1,0:T(8,128)(2,1)} %bitcast.183), kind=kOutput, calls=%fused_computation.49 | convolution fusion | flops 2147483648 | bytes 29360128 | tf_op jit(solution)/shard_map/nhts,nshd->nthd/dot_general | solution.py:136
  (133 shorter events, 205.4 us)
Async XLA Ops:
  24.6 10.7 %copy-start.5 = (bf16[128,8,16,128]{3,2,1,0:T(8,128)(2,1)}, bf16[128,8,16,128]{3,2,1,0:T(8,128)(2,1)S(1)}, u32[]{:S(2)}) copy-start(bf16[128,8,16,128]{3,2,1,0:T(8,128)(2,1)S(1)} %copy.116) | copy-start | bytes 12582916
  26.0 9.7 %copy-start.2 = (bf16[128,8,16,128]{3,2,1,0:T(8,128)(2,1)}, bf16[128,8,16,128]{3,2,1,0:T(8,128)(2,1)S(1)}, u32[]{:S(2)}) copy-start(bf16[128,8,16,128]{3,2,1,0:T(8,128)(2,1)S(1)} %copy.118) | copy-start | bytes 12582916
  37.0 15.4 %collective-permute-start = (f32[16,128,128]{2,1,0:T(8,128)S(1)}, f32[16,128,128]{2,1,0:T(8,128)S(1)}, u32[]{:S(2)}, u32[]{:S(2)}) collective-permute-start(f32[16,128,128]{2,1,0:T(8,128)S(1)} %get-tuple-element.169), channel_id=1, source_target_pairs={{0,4},{4,8},{8,12},{12,16},{16,20},{20,24},{24,28},{1,5},{5,9},{9,... | collective-permute-start | bytes 3145736 | tf_op jit(solution)/shard_map/while/body/eval_jaxpr/ppermute | solution.py:17
  53.4 17.0 %collective-permute-start = (f32[16,128,128]{2,1,0:T(8,128)S(1)}, f32[16,128,128]{2,1,0:T(8,128)S(1)}, u32[]{:S(2)}, u32[]{:S(2)}) collective-permute-start(f32[16,128,128]{2,1,0:T(8,128)S(1)} %get-tuple-element.169), channel_id=1, source_target_pairs={{0,4},{4,8},{8,12},{12,16},{16,20},{20,24},{24,28},{1,5},{5,9},{9,... | collective-permute-start | bytes 3145736 | tf_op jit(solution)/shard_map/while/body/eval_jaxpr/ppermute | solution.py:17
  71.4 17.0 %collective-permute-start = (f32[16,128,128]{2,1,0:T(8,128)S(1)}, f32[16,128,128]{2,1,0:T(8,128)S(1)}, u32[]{:S(2)}, u32[]{:S(2)}) collective-permute-start(f32[16,128,128]{2,1,0:T(8,128)S(1)} %get-tuple-element.169), channel_id=1, source_target_pairs={{0,4},{4,8},{8,12},{12,16},{16,20},{20,24},{24,28},{1,5},{5,9},{9,... | collective-permute-start | bytes 3145736 | tf_op jit(solution)/shard_map/while/body/eval_jaxpr/ppermute | solution.py:17
  89.3 17.0 %collective-permute-start = (f32[16,128,128]{2,1,0:T(8,128)S(1)}, f32[16,128,128]{2,1,0:T(8,128)S(1)}, u32[]{:S(2)}, u32[]{:S(2)}) collective-permute-start(f32[16,128,128]{2,1,0:T(8,128)S(1)} %get-tuple-element.169), channel_id=1, source_target_pairs={{0,4},{4,8},{8,12},{12,16},{16,20},{20,24},{24,28},{1,5},{5,9},{9,... | collective-permute-start | bytes 3145736 | tf_op jit(solution)/shard_map/while/body/eval_jaxpr/ppermute | solution.py:17
  107.3 17.0 %collective-permute-start = (f32[16,128,128]{2,1,0:T(8,128)S(1)}, f32[16,128,128]{2,1,0:T(8,128)S(1)}, u32[]{:S(2)}, u32[]{:S(2)}) collective-permute-start(f32[16,128,128]{2,1,0:T(8,128)S(1)} %get-tuple-element.169), channel_id=1, source_target_pairs={{0,4},{4,8},{8,12},{12,16},{16,20},{20,24},{24,28},{1,5},{5,9},{9,... | collective-permute-start | bytes 3145736 | tf_op jit(solution)/shard_map/while/body/eval_jaxpr/ppermute | solution.py:17
  125.3 17.0 %collective-permute-start = (f32[16,128,128]{2,1,0:T(8,128)S(1)}, f32[16,128,128]{2,1,0:T(8,128)S(1)}, u32[]{:S(2)}, u32[]{:S(2)}) collective-permute-start(f32[16,128,128]{2,1,0:T(8,128)S(1)} %get-tuple-element.169), channel_id=1, source_target_pairs={{0,4},{4,8},{8,12},{12,16},{16,20},{20,24},{24,28},{1,5},{5,9},{9,... | collective-permute-start | bytes 3145736 | tf_op jit(solution)/shard_map/while/body/eval_jaxpr/ppermute | solution.py:17
  143.3 17.0 %collective-permute-start = (f32[16,128,128]{2,1,0:T(8,128)S(1)}, f32[16,128,128]{2,1,0:T(8,128)S(1)}, u32[]{:S(2)}, u32[]{:S(2)}) collective-permute-start(f32[16,128,128]{2,1,0:T(8,128)S(1)} %get-tuple-element.169), channel_id=1, source_target_pairs={{0,4},{4,8},{8,12},{12,16},{16,20},{20,24},{24,28},{1,5},{5,9},{9,... | collective-permute-start | bytes 3145736 | tf_op jit(solution)/shard_map/while/body/eval_jaxpr/ppermute | solution.py:17
  205.1 10.3 %copy-start.14 = (f32[2048]{0:T(1024)S(1)}, f32[2048]{0:T(1024)}, u32[]{:S(2)}) copy-start(f32[2048]{0:T(1024)} %param.18) | copy-start | bytes 24580
  277.0 20.0 %collective-permute-start.1 = (f32[16,128,128]{2,1,0:T(8,128)}, f32[16,128,128]{2,1,0:T(8,128)S(1)}, u32[]{:S(2)}, u32[]{:S(2)}) collective-permute-start(f32[16,128,128]{2,1,0:T(8,128)} %get-tuple-element.187), channel_id=1, source_target_pairs={{4,0},{8,4},{12,8},{16,12},{20,16},{24,20},{28,24},{5,1},{9,5},{13... | collective-permute-start | bytes 3145736 | tf_op jit(solution)/shard_map/while/body/eval_jaxpr/ppermute | solution.py:17
  298.3 17.2 %collective-permute-start.1 = (f32[16,128,128]{2,1,0:T(8,128)}, f32[16,128,128]{2,1,0:T(8,128)S(1)}, u32[]{:S(2)}, u32[]{:S(2)}) collective-permute-start(f32[16,128,128]{2,1,0:T(8,128)} %get-tuple-element.187), channel_id=1, source_target_pairs={{4,0},{8,4},{12,8},{16,12},{20,16},{24,20},{28,24},{5,1},{9,5},{13... | collective-permute-start | bytes 3145736 | tf_op jit(solution)/shard_map/while/body/eval_jaxpr/ppermute | solution.py:17
  316.8 17.2 %collective-permute-start.1 = (f32[16,128,128]{2,1,0:T(8,128)}, f32[16,128,128]{2,1,0:T(8,128)S(1)}, u32[]{:S(2)}, u32[]{:S(2)}) collective-permute-start(f32[16,128,128]{2,1,0:T(8,128)} %get-tuple-element.187), channel_id=1, source_target_pairs={{4,0},{8,4},{12,8},{16,12},{20,16},{24,20},{28,24},{5,1},{9,5},{13... | collective-permute-start | bytes 3145736 | tf_op jit(solution)/shard_map/while/body/eval_jaxpr/ppermute | solution.py:17
  335.3 17.2 %collective-permute-start.1 = (f32[16,128,128]{2,1,0:T(8,128)}, f32[16,128,128]{2,1,0:T(8,128)S(1)}, u32[]{:S(2)}, u32[]{:S(2)}) collective-permute-start(f32[16,128,128]{2,1,0:T(8,128)} %get-tuple-element.187), channel_id=1, source_target_pairs={{4,0},{8,4},{12,8},{16,12},{20,16},{24,20},{28,24},{5,1},{9,5},{13... | collective-permute-start | bytes 3145736 | tf_op jit(solution)/shard_map/while/body/eval_jaxpr/ppermute | solution.py:17
  353.8 17.2 %collective-permute-start.1 = (f32[16,128,128]{2,1,0:T(8,128)}, f32[16,128,128]{2,1,0:T(8,128)S(1)}, u32[]{:S(2)}, u32[]{:S(2)}) collective-permute-start(f32[16,128,128]{2,1,0:T(8,128)} %get-tuple-element.187), channel_id=1, source_target_pairs={{4,0},{8,4},{12,8},{16,12},{20,16},{24,20},{28,24},{5,1},{9,5},{13... | collective-permute-start | bytes 3145736 | tf_op jit(solution)/shard_map/while/body/eval_jaxpr/ppermute | solution.py:17
  372.3 17.2 %collective-permute-start.1 = (f32[16,128,128]{2,1,0:T(8,128)}, f32[16,128,128]{2,1,0:T(8,128)S(1)}, u32[]{:S(2)}, u32[]{:S(2)}) collective-permute-start(f32[16,128,128]{2,1,0:T(8,128)} %get-tuple-element.187), channel_id=1, source_target_pairs={{4,0},{8,4},{12,8},{16,12},{20,16},{24,20},{28,24},{5,1},{9,5},{13... | collective-permute-start | bytes 3145736 | tf_op jit(solution)/shard_map/while/body/eval_jaxpr/ppermute | solution.py:17
  390.8 17.2 %collective-permute-start.1 = (f32[16,128,128]{2,1,0:T(8,128)}, f32[16,128,128]{2,1,0:T(8,128)S(1)}, u32[]{:S(2)}, u32[]{:S(2)}) collective-permute-start(f32[16,128,128]{2,1,0:T(8,128)} %get-tuple-element.187), channel_id=1, source_target_pairs={{4,0},{8,4},{12,8},{16,12},{20,16},{24,20},{28,24},{5,1},{9,5},{13... | collective-permute-start | bytes 3145736 | tf_op jit(solution)/shard_map/while/body/eval_jaxpr/ppermute | solution.py:17
  411.5 19.3 %copy-start.13 = (pred[2,512,512]{2,1,0:T(8,128)(4,1)S(1)}, pred[2,512,512]{2,1,0:T(8,128)(4,1)}, u32[]{:S(2)}) copy-start(pred[2,512,512]{2,1,0:T(8,128)(4,1)} %compare_and_fusion) | copy-start | bytes 1572868
  426.1 4.7 copy-start
  426.2 4.7 copy-start.3
  468.6 8.2 %copy-start.1 = (f32[2,16,512,128]{3,2,1,0:T(8,128)S(1)}, f32[2,16,512,128]{3,2,1,0:T(8,128)}, u32[]{:S(2)}) copy-start(f32[2,16,512,128]{3,2,1,0:T(8,128)} %fusion.40) | copy-start | bytes 25165828
  468.6 9.7 %copy-start.4 = (bf16[128,8,16,128]{3,2,1,0:T(8,128)(2,1)S(1)}, bf16[128,8,16,128]{3,2,1,0:T(8,128)(2,1)}, u32[]{:S(2)}) copy-start(bf16[128,8,16,128]{3,2,1,0:T(8,128)(2,1)} %copy-done.2) | copy-start | bytes 12582916
  494.6 6.6 %copy-start.8 = (bf16[2,512,16,128]{3,2,1,0:T(8,128)(2,1)S(1)}, bf16[2,512,16,128]{3,2,1,0:T(8,128)(2,1)}, u32[]{:S(2)}) copy-start(bf16[2,512,16,128]{3,2,1,0:T(8,128)(2,1)} %copy.102) | copy-start | bytes 12582916
  494.6 6.6 %copy-start.9 = (bf16[2,512,16,128]{3,2,1,0:T(8,128)(2,1)S(1)}, bf16[2,512,16,128]{3,2,1,0:T(8,128)(2,1)}, u32[]{:S(2)}) copy-start(bf16[2,512,16,128]{3,2,1,0:T(8,128)(2,1)} %copy.96) | copy-start | bytes 12582916
  (17 other events, 22.7 us)
where the time goes:
time: 513 us; the launch traced here: 508 us
  waiting for transfers between devices  192 us (37%)
  matrix products  132 us (26%)
  local copies, waits for them, and re-layouts  83.5 us (16%)
  starting transfers between devices  48.7 us (9%)
  other arithmetic  40.9 us (8%)
  blocking collectives  10.1 us (2%)
    ppermute x14, waiting for transfers between devices, passed_along(): return lax.ppermute(block, axis, route)  192 us
    ppermute x14, starting transfers between devices, passed_along(): return lax.ppermute(block, axis, route)  48.7 us
    unnamed x36, local copies, waits for them, and re-layouts  24.8 us
    dot_general x1, matrix products, body(): jnp.einsum('nthd,nshd->nhts', query_block, key_block, preferred_element_t...  19.6 us
    dot_general x1, matrix products, body(): jnp.einsum('nshd,nhde->nshe', key_block, back_held, preferred_element_typ...  14.6 us
    dot_general x1, matrix products, body(): jnp.einsum('nthe,nshe->nhts', agrad_block, value_block, preferred_element...  14 us
    unnamed x2, other arithmetic  13.2 us
    dot_general x1, matrix products, body(): jnp.einsum('nhts,nshe->nthe', weights_bf, value_block, preferred_element_...  12.7 us
  transfers between devices with their start and end apart: 14, of which 14 were waited for; matrix products, arithmetic and copies ran while one was open for 0% of the time, Pallas kernels for 0%

commit v1 on v0

v1 whole, which is shorter than its diff:
```python
import functools

import jax
import jax.numpy as jnp
from jax import lax
from jax.experimental import pallas as pl
from jax.experimental.pallas import tpu as pltpu
from jax.sharding import PartitionSpec as P

HEAD_TOTAL = 64
HD = 128
CHUNK = 256
GROUP = 2
WIDTH = HEAD_TOTAL * HD

epsilon = 1e-06
LOG2E = 1.4426950408889634

F32 = jnp.float32
BF16 = jnp.bfloat16
MIB = 1024 * 1024


def dot(a, b, dims=((1,), (0,))):
    return lax.dot_general(a, b, (dims, ((), ())), preferred_element_type=F32)


NT = ((1,), (1,))


def column(row):
    return jnp.broadcast_to(row, (HD, row.shape[1])).T


def wide(col):
    return jnp.concatenate([col] * (CHUNK // HD), axis=1)


def chunk_cumsum(x):
    lane = lax.broadcasted_iota(jnp.int32, x.shape, 1) % CHUNK
    shift = 1
    while shift < CHUNK:
        x = x + jnp.where(lane >= shift, pltpu.roll(x, shift, 1), 0.0)
        shift *= 2
    return x


def fill_masks(rrow_ref, mask_ref, transposed):
    for n in range(mask_ref.shape[0]):
        r_row = rrow_ref[0:1, n * CHUNK : (n + 1) * CHUNK]
        r_col = wide(column(r_row))
        sub = lax.broadcasted_iota(jnp.int32, (CHUNK, CHUNK), 0)
        lane = lax.broadcasted_iota(jnp.int32, (CHUNK, CHUNK), 1)
        causal = (sub <= lane) if transposed else (lane <= sub)
        mask_ref[n] = jnp.where((r_col == r_row) & causal, 0.0, -jnp.inf)


def state_kernel(
    chunks, piece, lc_ref, doc_ref, k_ref, v_ref,
    crow_ref, enter_ref, leave_ref, rrow_ref, loc_ref, sext_ref,
):
    step = pl.program_id(0)

    @pl.when(step == 0)
    def _():
        c = chunk_cumsum(lc_ref[...] * LOG2E)
        r = chunk_cumsum(jnp.broadcast_to(doc_ref[...].astype(F32), (8, doc_ref.shape[1])))
        crow_ref[...] = c
        rrow_ref[...] = r
        r1 = r[0:1]
        enter_ref[...] = jnp.where(r1 == 0.0, jnp.exp2(c), 0.0)
        for n in range(chunks):
            span = slice(n * CHUNK, (n + 1) * CHUNK)
            cn, rn = c[:, span], r1[:, span]
            leave_ref[:, span] = jnp.where(
                rn == rn[:, -1:], jnp.exp2(cn[:, -1:] - cn), 0.0
            )

    for g in range(GROUP):
        h = step * GROUP + g
        cols = slice(g * HD, (g + 1) * HD)
        state = None
        total = None
        for n in range(chunks):
            span = slice(n * CHUNK, (n + 1) * CHUNK)
            keyed = (k_ref[span, cols].T.astype(F32) * leave_ref[pl.ds(h, 1), span]).astype(BF16)
            local = dot(keyed, v_ref[span, cols])
            loc_ref[g, n] = local
            passing = enter_ref[pl.ds(h, 1), span][:, CHUNK - 1 : CHUNK]
            state = local if state is None else passing * state + local
            total = passing if total is None else passing * total
        for i in range(HD // piece):
            at = g * (HD // piece) + i
            sext_ref[at, 0:piece, :] = state[i * piece : (i + 1) * piece]
            sext_ref[at, piece : piece + 8, :] = jnp.broadcast_to(total, (8, HD))


def inside_kernel(chunks, rrow_ref, crow_ref, q_ref, k_ref, v_ref, out_ref, mask_ref):
    step = pl.program_id(0)

    @pl.when(step == 0)
    def _():
        fill_masks(rrow_ref, mask_ref, False)

    for g in range(GROUP):
        h = step * GROUP + g
        cols = slice(g * HD, (g + 1) * HD)
        for n in range(chunks):
            span = slice(n * CHUNK, (n + 1) * CHUNK)
            c_row = crow_ref[pl.ds(h, 1), span]
            weight = jnp.exp2(wide(column(c_row)) - c_row + mask_ref[n])
            scores = dot(q_ref[span, cols], k_ref[span, cols], NT)
            probs = (scores * weight).astype(BF16)
            out_ref[span, cols] = dot(probs, v_ref[span, cols])


def outside_kernel(
    chunks, enter_ref, gain_ref, q_ref, gate_ref, grad_ref, inside_ref, loc_ref, in_ref,
    attn_ref, held_ref, sums_ref, sq_ref, inner_ref,
):
    step = pl.program_id(0)

    @pl.when(step == 0)
    def _():
        sq_ref[...] = jnp.zeros_like(sq_ref)
        inner_ref[...] = jnp.zeros_like(inner_ref)

    for g in range(GROUP):
        h = step * GROUP + g
        cols = slice(g * HD, (g + 1) * HD)
        gain = gain_ref[0:1, cols]
        carry = in_ref[g]
        for n in range(chunks):
            span = slice(n * CHUNK, (n + 1) * CHUNK)
            enter = enter_ref[pl.ds(h, 1), span]
            held = carry.astype(BF16)
            held_ref[g, n] = held
            attn = inside_ref[span, cols] + column(enter) * dot(q_ref[span, cols], held)
            attn_ref[span, cols] = attn
            sig = jax.nn.sigmoid(gate_ref[span, cols].astype(F32))
            gnorm = grad_ref[span, cols].astype(F32) * sig
            sq_ref[span, :] += attn * attn
            inner_ref[span, :] += gnorm * gain * attn
            if n + 1 < chunks:
                carry = enter[:, CHUNK - 1 : CHUNK] * carry + loc_ref[g, n]

    @pl.when(step == pl.num_programs(0) - 1)
    def _():
        sums_ref[0:1, :] = jnp.sum(sq_ref[...].T, axis=0, keepdims=True)
        sums_ref[1:2, :] = jnp.sum(inner_ref[...].T, axis=0, keepdims=True)


def grad_kernel(
    chunks, piece, parts, enter_ref, gain_ref, *refs,
):
    sums_refs = refs[:parts]
    q_ref, gate_ref, grad_ref, attn_ref = refs[parts : parts + 4]
    gated_ref, ggate_ref, agrad_ref, bloc_ref, dback_ref, alpha_ref, beta_ref = refs[parts + 4 :]
    step = pl.program_id(0)

    @pl.when(step == 0)
    def _():
        sums = sums_refs[0][...]
        for ref in sums_refs[1:]:
            sums = sums + ref[...]
        inverse = lax.rsqrt(sums[0:1] / WIDTH + epsilon)
        alpha_ref[...] = column(inverse)
        beta_ref[...] = column(inverse * inverse * inverse * sums[1:2] / WIDTH)

    for g in range(GROUP):
        h = step * GROUP + g
        cols = slice(g * HD, (g + 1) * HD)
        gain = gain_ref[0:1, cols]
        back = None
        for n in reversed(range(chunks)):
            span = slice(n * CHUNK, (n + 1) * CHUNK)
            enter = enter_ref[pl.ds(h, 1), span]
            attn = attn_ref[span, cols]
            sig = jax.nn.sigmoid(gate_ref[span, cols].astype(F32))
            grad = grad_ref[span, cols].astype(F32)
            scale = alpha_ref[span, :] * gain
            gated = attn * scale * sig
            gated_ref[span, cols] = gated.astype(BF16)
            ggate_ref[span, cols] = (grad * gated * (1.0 - sig)).astype(BF16)
            agrad = (scale * (grad * sig) - attn * beta_ref[span, :]).astype(BF16)
            agrad_ref[span, cols] = agrad
            qkeyed = (q_ref[span, cols].T.astype(F32) * enter).astype(BF16)
            local = dot(qkeyed, agrad)
            bloc_ref[g, n] = local
            back = local if back is None else local + enter[:, CHUNK - 1 : CHUNK] * back
        for i in range(HD // piece):
            dback_ref[g * (HD // piece) + i] = back[i * piece : (i + 1) * piece]


def inner_grad_kernel(
    chunks, rrow_ref, crow_ref, enter_ref, q_ref, k_ref, v_ref, agrad_ref, held_ref,
    dq_ref, dk_ref, dv_ref, mask_ref,
):
    step = pl.program_id(0)

    @pl.when(step == 0)
    def _():
        fill_masks(rrow_ref, mask_ref, True)

    for g in range(GROUP):
        h = step * GROUP + g
        cols = slice(g * HD, (g + 1) * HD)
        for n in range(chunks):
            span = slice(n * CHUNK, (n + 1) * CHUNK)
            c_row = crow_ref[pl.ds(h, 1), span]
            q, k = q_ref[span, cols], k_ref[span, cols]
            v, agrad = v_ref[span, cols], agrad_ref[span, cols]
            weight = jnp.exp2(c_row - wide(column(c_row)) + mask_ref[n])
            probs = (dot(k, q, NT) * weight).astype(BF16)
            dv_ref[span, cols] = dot(probs, agrad).astype(dv_ref.dtype)
            dscore = (dot(v, agrad, NT) * weight).astype(BF16)
            dk_ref[span, cols] = dot(dscore, q).astype(dk_ref.dtype)
            outside = column(enter_ref[pl.ds(h, 1), span]) * dot(agrad, held_ref[g, n], NT)
            dq_ref[span, cols] = (dot(dscore.T, k) + outside).astype(BF16)


def outer_grad_kernel(
    chunks, enter_ref, leave_ref, k_ref, v_ref, dkin_ref, dvin_ref, bloc_ref, out_ref,
    dk_ref, dv_ref,
):
    step = pl.program_id(0)
    for g in range(GROUP):
        h = step * GROUP + g
        cols = slice(g * HD, (g + 1) * HD)
        carry = out_ref[g]
        for n in reversed(range(chunks)):
            span = slice(n * CHUNK, (n + 1) * CHUNK)
            leave = column(leave_ref[pl.ds(h, 1), span])
            back = carry.astype(BF16)
            dk = dkin_ref[span, cols].astype(F32) + leave * dot(v_ref[span, cols], back, NT)
            dv = dvin_ref[span, cols].astype(F32) + leave * dot(k_ref[span, cols], back)
            dk_ref[span, cols] = dk.astype(BF16)
            dv_ref[span, cols] = dv.astype(BF16)
            if n > 0:
                passing = enter_ref[pl.ds(h, 1), span][:, CHUNK - 1 : CHUNK]
                carry = bloc_ref[g, n] + passing * carry


def prefix_kernel(devices, piece, ext_ref, out_ref):
    carry = jnp.zeros((piece, HD), F32)
    for d in range(devices):
        out_ref[d, 0] = carry
        if d + 1 < devices:
            carry = ext_ref[d, 0, piece : piece + 1, :] * carry + ext_ref[d, 0, 0:piece, :]


def suffix_kernel(devices, pass_ref, back_ref, out_ref):
    carry = jnp.zeros(back_ref.shape[2:], F32)
    for d in reversed(range(devices)):
        out_ref[d, 0] = carry
        if d > 0:
            carry = back_ref[d, 0] + pass_ref[d, 0, 0:1, :] * carry


def call(kernel, grid, in_specs, out_specs, out_shape, scratch=(), flops=0, moved=0, exps=0):
    return pl.pallas_call(
        kernel,
        grid=grid,
        in_specs=in_specs,
        out_specs=out_specs,
        out_shape=out_shape,
        scratch_shapes=list(scratch),
        compiler_params=pltpu.CompilerParams(
            dimension_semantics=("arbitrary",) * len(grid), vmem_limit_bytes=40 * MIB
        ),
        cost_estimate=pl.CostEstimate(flops=flops, bytes_accessed=moved, transcendentals=exps),
    )


def shape(dims, dtype):
    return jax.ShapeDtypeStruct(dims, dtype)


def body(queries, key_rows, value_rows, log_decay, doc_start, gate_input, norm_gain, out_grad):
    rows, cols = queries.shape
    heads = cols // HD
    chunks = rows // CHUNK
    devices = lax.axis_size("seq")
    parts = lax.axis_size("head")
    piece = min(HD, heads * HD // devices)
    per = HD // piece
    own = heads * per // devices
    grid = (heads // GROUP,)
    big = rows * cols * 2
    tile = 2 * rows * CHUNK * cols
    small = 2 * rows * HD * cols

    whole = lambda *dims: pl.BlockSpec(dims, lambda i: (0,) * len(dims))
    wide_spec = pl.BlockSpec((rows, GROUP * HD), lambda i: (0, i))
    row_spec = whole(heads, rows)
    rrow_spec = whole(8, rows)
    loc_spec = pl.BlockSpec((GROUP, chunks, HD, HD), lambda i: (i, 0, 0, 0))
    state_spec = pl.BlockSpec((GROUP, HD, HD), lambda i: (i, 0, 0))
    gain_spec = pl.BlockSpec((1, GROUP * HD), lambda i: (0, i))
    mask = pltpu.VMEM((chunks, CHUNK, CHUNK), F32)
    tall = pltpu.VMEM((rows, HD), F32)

    row_shape = shape((heads, rows), F32)
    loc_shape = shape((heads, chunks, HD, HD), F32)
    big_shape = shape((rows, cols), BF16)

    doc_row = doc_start.reshape(1, rows)
    gain_row = norm_gain.reshape(1, cols)

    crow, enter, leave, rrow, loc, sext = call(
        functools.partial(state_kernel, chunks, piece),
        grid,
        [row_spec, whole(1, rows), wide_spec, wide_spec],
        [
            row_spec, row_spec, row_spec, rrow_spec, loc_spec,
            pl.BlockSpec((GROUP * per, piece + 8, HD), lambda i: (i, 0, 0)),
        ],
        [
            row_shape, row_shape, row_shape, shape((8, rows), F32), loc_shape,
            shape((heads * per, piece + 8, HD), F32),
        ],
        flops=small, moved=2 * big + 6 * MIB,
    )(log_decay, doc_row, key_rows, value_rows)

    ext = lax.all_to_all(sext.reshape(devices, own, piece + 8, HD), "seq", 0, 0)

    inside = call(
        functools.partial(inside_kernel, chunks),
        grid,
        [rrow_spec, row_spec, wide_spec, wide_spec, wide_spec],
        wide_spec,
        shape((rows, cols), F32),
        [mask],
        flops=2 * tile, moved=5 * big, exps=rows * CHUNK * heads,
    )(rrow, crow, queries, key_rows, value_rows)

    scan_spec = pl.BlockSpec((devices, 1, piece, HD), lambda i: (0, i, 0, 0))
    before = call(
        functools.partial(prefix_kernel, devices, piece),
        (own,),
        [pl.BlockSpec((devices, 1, piece + 8, HD), lambda i: (0, i, 0, 0))],
        scan_spec,
        shape((devices, own, piece, HD), F32),
        moved=2 * MIB,
    )(ext)
    incoming = lax.all_to_all(before, "seq", 0, 0).reshape(heads, HD, HD)

    attn, held, sums = call(
        functools.partial(outside_kernel, chunks),
        grid,
        [row_spec, gain_spec, wide_spec, wide_spec, wide_spec, wide_spec, loc_spec, state_spec],
        [wide_spec, loc_spec, whole(2, rows)],
        [shape((rows, cols), F32), shape((heads, chunks, HD, HD), BF16), shape((2, rows), F32)],
        [tall, tall],
        flops=small, moved=7 * big + 6 * MIB, exps=rows * cols,
    )(enter, gain_row, queries, gate_input, out_grad, inside, loc, incoming)

    all_sums = [sums]
    for hop in range(1, parts):
        route = [(i, (i + hop) % parts) for i in range(parts)]
        all_sums.append(lax.ppermute(sums, "head", route))

    gated, gate_grad, agrad, bloc, dback = call(
        functools.partial(grad_kernel, chunks, piece, parts),
        grid,
        [row_spec, gain_spec] + [whole(2, rows)] * parts + [wide_spec] * 4,
        [
            wide_spec, wide_spec, wide_spec, loc_spec,
            pl.BlockSpec((GROUP * per, piece, HD), lambda i: (i, 0, 0)),
        ],
        [big_shape, big_shape, big_shape, loc_shape, shape((heads * per, piece, HD), F32)],
        [tall, tall],
        flops=small, moved=8 * big + 5 * MIB, exps=rows * cols,
    )(enter, gain_row, *all_sums, queries, gate_input, out_grad, attn)

    backs = lax.all_to_all(dback.reshape(devices, own, piece, HD), "seq", 0, 0)

    dq, dk_inner, dv_inner = call(
        functools.partial(inner_grad_kernel, chunks),
        grid,
        [rrow_spec, row_spec, row_spec] + [wide_spec] * 4 + [loc_spec],
        [wide_spec] * 3,
        [big_shape] * 3,
        [mask],
        flops=5 * tile + small, moved=7 * big + 2 * MIB, exps=rows * CHUNK * heads,
    )(rrow, crow, enter, queries, key_rows, value_rows, agrad, held)

    after = call(
        functools.partial(suffix_kernel, devices),
        (own,),
        [pl.BlockSpec((devices, 1, 8, HD), lambda i: (0, i, piece // 8, 0)), scan_spec],
        scan_spec,
        shape((devices, own, piece, HD), F32),
        moved=2 * MIB,
    )(ext, backs)
    outgoing = lax.all_to_all(after, "seq", 0, 0).reshape(heads, HD, HD)

    dk, dv = call(
        functools.partial(outer_grad_kernel, chunks),
        grid,
        [row_spec, row_spec] + [wide_spec] * 4 + [loc_spec, state_spec],
        [wide_spec] * 2,
        [big_shape] * 2,
        flops=2 * small, moved=6 * big + 5 * MIB,
    )(enter, leave, key_rows, value_rows, dk_inner, dv_inner, bloc, outgoing)
    return (gated, gate_grad, dq, dk, dv)


def solution(mesh):
    in_specs = (
        P("seq", "head"),
        P("seq", "head"),
        P("seq", "head"),
        P("head", "seq"),
        P("seq"),
        P("seq", "head"),
        P("head"),
        P("seq", "head"),
    )
    out_specs = (P("seq", "head"),) * 5
    return jax.shard_map(body, mesh=mesh, in_specs=in_specs, out_specs=out_specs, check_vma=False)
```

time: 513 us -> 172 us (0.34)
  the two profiles are of different devices: /device:TPU:3 before, /device:TPU:0 now
where the time goes in v1:
time: 172 us; the launch traced here: 171 us
  Pallas kernels  77.4 us (45%)
  blocking collectives  40.3 us (23%)
  local copies, waits for them, and re-layouts  36.3 us (21%)
  starting transfers between devices  11.8 us (7%)
  waiting for transfers between devices  4.42 us (3%)
    unnamed x40, local copies, waits for them, and re-layouts  36.3 us
    pallas_call x1, Pallas kernels, body(): call(functools.partial(inner_grad_kernel, chunks), grid, [rrow_spec, row_...  23.3 us
    all_to_all x1, blocking collectives, body(): ext = lax.all_to_all(sext.reshape(devices, own, piece + 8, HD), 'seq', 0, 0)  21 us
    all_to_all x1, blocking collectives, body(): backs = lax.all_to_all(dback.reshape(devices, own, piece, HD), 'seq', 0, 0)  19.3 us
    pallas_call x1, Pallas kernels, body(): call(functools.partial(outside_kernel, chunks), grid, [row_spec, gain_spe...  13.2 us
    pallas_call x1, Pallas kernels, body(): call(functools.partial(grad_kernel, chunks, piece, parts), grid, [row_spe...  13 us
    pallas_call x1, Pallas kernels, body(): call(functools.partial(inside_kernel, chunks), grid, [rrow_spec, row_spec...  10.7 us
    pallas_call x1, Pallas kernels, body(): call(functools.partial(outer_grad_kernel, chunks), grid, [row_spec, row_s...  10.2 us
  transfers between devices with their start and end apart: 5, of which 3 were waited for; matrix products, arithmetic and copies ran while one was open for 0% of the time, Pallas kernels for 20%

profile of v1, /device:TPU:0, one launch (start us, length us, event | category | flops | bytes accessed | tf_op | source)
XLA Modules:
  0.0 170.9 jit_solution(3354521994579017614)
XLA Ops:
  0.6 2.2 %copy-done.2 = bf16[1024,2048]{1,0:T(8,128)(2,1)S(1)} copy-done((bf16[1024,2048]{1,0:T(8,128)(2,1)S(1)}, bf16[1024,2048]{1,0:T(8,128)(2,1)}, u32[]{:S(2)}) %copy-start.2) | copy-done | bytes 4194328
  2.8 2.2 %copy-done.5 = bf16[1024,2048]{1,0:T(8,128)(2,1)S(1)} copy-done((bf16[1024,2048]{1,0:T(8,128)(2,1)S(1)}, bf16[1024,2048]{1,0:T(8,128)(2,1)}, u32[]{:S(2)}) %copy-start.5) | copy-done | bytes 4194328
  6.5 4.8 %shard_map.119 = (f32[16,1024]{1,0:T(8,128)S(1)}, f32[16,1024]{1,0:T(8,128)S(1)}, f32[16,1024]{1,0:T(8,128)S(1)}, f32[8,1024]{1,0:T(8,128)S(1)}, f32[16,4,128,12...) custom-call(f32[16,1024]{1,0:T(8,128)S(1)} %copy-done.14, s32[1,1024]{1,0:T(1,128)S(1)} %bitcast.12, ...), custom_call_target="tpu_custom_call" | custom-call | flops 536870912 | bytes 14680064 | tf_op jit(solution)/shard_map/pallas_call | solution.py:310
  13.3 21.0 %all_to_all.20.ext_ref.pass_ref = f32[8,2,136,128]{3,2,1,0:T(8,128)S(1)} all-to-all(f32[8,2,136,128]{3,2,1,0:T(8,128)S(1)} %bitcast.8), channel_id=1, replica_groups=mesh['seq'=8,'head'=4] {'seq'}, dimensions={0} | all-to-all | bytes 2228224 | tf_op jit(solution)/shard_map/all_to_all | solution.py:325
  35.4 3.6 %all-to-all-start.1 = ((f32[8,2,128,128]{3,2,1,0:T(8,128)}), f32[8,2,128,128]{3,2,1,0:T(8,128)S(1)}, u32[]{:S(2)}, u32[]{:S(2)}) async-start(f32[8,2,128,128]{3,2,1,0:T(8,128)} %shard_map.121), calls=%async_computation.1 | async-start | bytes 2097152 | tf_op jit(solution)/shard_map/all_to_all | solution.py:346
  39.0 2.2 %copy-done = bf16[1024,2048]{1,0:T(8,128)(2,1)S(1)} copy-done((bf16[1024,2048]{1,0:T(8,128)(2,1)S(1)}, bf16[1024,2048]{1,0:T(8,128)(2,1)}, u32[]{:S(2)}) %copy-start) | copy-done | bytes 4194328
  41.2 2.2 %copy-done.3 = bf16[1024,2048]{1,0:T(8,128)(2,1)S(1)} copy-done((bf16[1024,2048]{1,0:T(8,128)(2,1)S(1)}, bf16[1024,2048]{1,0:T(8,128)(2,1)}, u32[]{:S(2)}) %copy-start.3) | copy-done | bytes 4194328
  43.4 2.2 %copy-done.6 = bf16[1024,2048]{1,0:T(8,128)(2,1)S(1)} copy-done((bf16[1024,2048]{1,0:T(8,128)(2,1)S(1)}, bf16[1024,2048]{1,0:T(8,128)(2,1)}, u32[]{:S(2)}) %copy-start.6) | copy-done | bytes 4194328
  45.5 10.7 %shard_map.120.inside_ref = f32[1024,2048]{1,0:T(8,128)} custom-call(f32[8,1024]{1,0:T(8,128)S(1)} %get-tuple-element.25.rrow_ref, f32[16,1024]{1,0:T(8,128)S(1)} %get-tuple-element.26.crow_ref, bf16[1024,2048]{1,0:T(8,128)(2,1)S(1)} %copy-done, bf16[1024,2048]{1,0:T(8,128)(2,1)S(1)} %copy-done.3, bf16[1024,2048]{1,0:T(8,128)(2,1)S(1)} %copy-done.6), custom_call_target="tpu_custom_call" | custom-call | flops 2147483648 | bytes 20971520 | tf_op jit(solution)/shard_map/pallas_call | solution.py:327
  56.2 2.2 %copy-done.1 = bf16[1024,2048]{1,0:T(8,128)(2,1)S(1)} copy-done((bf16[1024,2048]{1,0:T(8,128)(2,1)S(1)}, bf16[1024,2048]{1,0:T(8,128)(2,1)}, u32[]{:S(2)}) %copy-start.1) | copy-done | bytes 4194328
  58.4 2.2 %copy-done.8 = bf16[1024,2048]{1,0:T(8,128)(2,1)S(1)} copy-done((bf16[1024,2048]{1,0:T(8,128)(2,1)S(1)}, bf16[1024,2048]{1,0:T(8,128)(2,1)}, u32[]{:S(2)}) %copy-start.8) | copy-done | bytes 4194328
  60.6 13.2 %shard_map.122 = (f32[1024,2048]{1,0:T(8,128)}, bf16[16,4,128,128]{3,2,1,0:T(8,128)(2,1)S(1)}, f32[2,1024]{1,0:T(2,128)S(1)}) custom-call(f32[16,1024]{1,0:T(8,128)S(1)} %get-tuple-element.24.enter_ref, f32[1,2048]{1,0:T(1,128)S(1)} %bitcast.10, bf16[1024,2048]{1,0:T(8,128)(2,1)S(1)} %copy-done.1, bf16[1024,2048]{1,0:T(8,128)(2,1)S(1)} %copy-done.8, ...), custom_call_target="tpu_custom_call" | custom-call | flops 536870912 | bytes 35651584 | tf_op jit(solution)/shard_map/pallas_call | solution.py:348
  75.1 3.6 %collective-permute-start.2 = (f32[2,1024]{1,0:T(2,128)S(1)}, f32[2,1024]{1,0:T(2,128)S(1)}, u32[]{:S(2)}, u32[]{:S(2)}) collective-permute-start(f32[2,1024]{1,0:T(2,128)S(1)} %get-tuple-element.29.refs_0_), channel_id=1, source_target_pairs={{0,3},{1,0},{2,1},{3,2},{4,7},{5,4},{6,5},{7,6},{8,11},{9,8},{10,9... | collective-permute-start | bytes 24584 | tf_op jit(solution)/shard_map/ppermute | solution.py:361
  80.0 3.2 %collective-permute-done.1.refs_2_ = f32[2,1024]{1,0:T(2,128)S(1)} collective-permute-done((f32[2,1024]{1,0:T(2,128)S(1)}, f32[2,1024]{1,0:T(2,128)S(1)}, u32[]{:S(2)}, u32[]{:S(2)}) %collective-permute-start.1) | collective-permute-done | bytes 8224 | tf_op jit(solution)/shard_map/ppermute | solution.py:361
  84.1 13.0 %shard_map.123 = (bf16[1024,2048]{1,0:T(8,128)(2,1)}, bf16[1024,2048]{1,0:T(8,128)(2,1)}, bf16[1024,2048]{1,0:T(8,128)(2,1)S(1)}, f32[16,4,128,128]{3,2,1,0:T(8,128)S(1)}, f32[16,128,128]{2,1,0:T(8,128)S(1)}) custom-call(f32[16,1024]{1,0:T(8,128)S(1)} %get-tuple-element.24.enter_ref, f32[1,2048]{1,0:T(1,128)S(1)} %bitcast.11, ...), custom_call_target="tpu_custom_call" | custom-call | flops 536870912 | bytes 38797312 | tf_op jit(solution)/shard_map/pallas_call | solution.py:363
  99.1 2.0 %copy-done.17 = bf16[1024,2048]{1,0:T(8,128)(2,1)} copy-done((bf16[1024,2048]{1,0:T(8,128)(2,1)}, bf16[1024,2048]{1,0:T(8,128)(2,1)S(1)}, u32[]{:S(2)}) %copy-start.17) | copy-done | bytes 4194328
  101.2 19.3 %all_to_all.21.back_ref = f32[8,2,128,128]{3,2,1,0:T(8,128)S(1)} all-to-all(f32[8,2,128,128]{3,2,1,0:T(8,128)S(1)} %bitcast.9), channel_id=1, replica_groups=mesh['seq'=8,'head'=4] {'seq'}, dimensions={0} | all-to-all | bytes 2097152 | tf_op jit(solution)/shard_map/all_to_all | solution.py:376
  121.6 3.6 %all-to-all-start.3 = ((f32[8,2,128,128]{3,2,1,0:T(8,128)}), f32[8,2,128,128]{3,2,1,0:T(8,128)S(1)}, u32[]{:S(2)}, u32[]{:S(2)}) async-start(f32[8,2,128,128]{3,2,1,0:T(8,128)} %shard_map.125), calls=%async_computation.3 | async-start | bytes 2097152 | tf_op jit(solution)/shard_map/all_to_all | solution.py:396
  126.8 23.3 %shard_map.124 = (bf16[1024,2048]{1,0:T(8,128)(2,1)}, bf16[1024,2048]{1,0:T(8,128)(2,1)S(1)}, bf16[1024,2048]{1,0:T(8,128)(2,1)S(1)}) custom-call(f32[8,1024]{1,0:T(8,128)S(1)} %get-tuple-element.25.rrow_ref, f32[16,1024]{1,0:T(8,128)S(1)} %get-tuple-element.26.crow_ref, f32[16,1024]{1,0:T(8,128)S(1)} %get-tuple-element.24.enter_ref, ...), custom_call_target="tpu_custom_call" | custom-call | flops 5905580032 | bytes 31457280 | tf_op jit(solution)/shard_map/pallas_call | solution.py:378
  152.1 2.0 %copy-done.13 = bf16[1024,2048]{1,0:T(8,128)(2,1)} copy-done((bf16[1024,2048]{1,0:T(8,128)(2,1)}, bf16[1024,2048]{1,0:T(8,128)(2,1)S(1)}, u32[]{:S(2)}) %copy-start.13) | copy-done | bytes 4194328
  154.1 2.2 %copy-done.4 = bf16[1024,2048]{1,0:T(8,128)(2,1)S(1)} copy-done((bf16[1024,2048]{1,0:T(8,128)(2,1)S(1)}, bf16[1024,2048]{1,0:T(8,128)(2,1)}, u32[]{:S(2)}) %copy-start.4) | copy-done | bytes 4194328
  156.3 2.2 %copy-done.7 = bf16[1024,2048]{1,0:T(8,128)(2,1)S(1)} copy-done((bf16[1024,2048]{1,0:T(8,128)(2,1)S(1)}, bf16[1024,2048]{1,0:T(8,128)(2,1)}, u32[]{:S(2)}) %copy-start.7) | copy-done | bytes 4194328
  158.5 2.2 %copy-done.12 = bf16[1024,2048]{1,0:T(8,128)(2,1)S(1)} copy-done((bf16[1024,2048]{1,0:T(8,128)(2,1)S(1)}, bf16[1024,2048]{1,0:T(8,128)(2,1)}, u32[]{:S(2)}) %copy-start.12) | copy-done | bytes 4194328
  160.6 10.2 %shard_map.126 = (bf16[1024,2048]{1,0:T(8,128)(2,1)}, bf16[1024,2048]{1,0:T(8,128)(2,1)}) custom-call(f32[16,1024]{1,0:T(8,128)S(1)} %get-tuple-element.24.enter_ref, f32[16,1024]{1,0:T(8,128)S(1)} %get-tuple-element.36.leave_ref, bf16[1024,2048]{1,0:T(8,128)(2,1)S(1)} %copy-done.4, bf16[1024,2048]{1,0:T(8,128)(2,1)S(1)} %copy-done.7, ...), custom_call_target="tpu_custom_call" | custom-call | flops 1073741824 | bytes 30408704 | tf_op jit(solution)/shard_map/pallas_call | solution.py:398
  (36 shorter events, 15.0 us)
Async XLA Ops:
  0.6 2.2 %copy-start.2 = (bf16[1024,2048]{1,0:T(8,128)(2,1)S(1)}, bf16[1024,2048]{1,0:T(8,128)(2,1)}, u32[]{:S(2)}) copy-start(bf16[1024,2048]{1,0:T(8,128)(2,1)} %k_ref.7) | copy-start | bytes 12582916
  2.8 2.2 %copy-start.5 = (bf16[1024,2048]{1,0:T(8,128)(2,1)S(1)}, bf16[1024,2048]{1,0:T(8,128)(2,1)}, u32[]{:S(2)}) copy-start(bf16[1024,2048]{1,0:T(8,128)(2,1)} %v_ref.7) | copy-start | bytes 12582916
  5.0 0.8 copy-start.14
  11.3 2.0 %copy-start.10 = (f32[16,4,128,128]{3,2,1,0:T(8,128)}, f32[16,4,128,128]{3,2,1,0:T(8,128)S(1)}, u32[]{:S(2)}) copy-start(f32[16,4,128,128]{3,2,1,0:T(8,128)S(1)} %get-tuple-element.27.loc_ref) | copy-start | bytes 12582916
  35.4 20.8 %all-to-all-start.1 = ((f32[8,2,128,128]{3,2,1,0:T(8,128)}), f32[8,2,128,128]{3,2,1,0:T(8,128)S(1)}, u32[]{:S(2)}, u32[]{:S(2)}) async-start(f32[8,2,128,128]{3,2,1,0:T(8,128)} %shard_map.121), calls=%async_computation.1 | async-start | bytes 2097152 | tf_op jit(solution)/shard_map/all_to_all | solution.py:346
  39.0 2.2 %copy-start = (bf16[1024,2048]{1,0:T(8,128)(2,1)S(1)}, bf16[1024,2048]{1,0:T(8,128)(2,1)}, u32[]{:S(2)}) copy-start(bf16[1024,2048]{1,0:T(8,128)(2,1)} %q_ref.5) | copy-start | bytes 12582916
  41.2 2.2 %copy-start.3 = (bf16[1024,2048]{1,0:T(8,128)(2,1)S(1)}, bf16[1024,2048]{1,0:T(8,128)(2,1)}, u32[]{:S(2)}) copy-start(bf16[1024,2048]{1,0:T(8,128)(2,1)} %k_ref.7) | copy-start | bytes 12582916
  43.4 2.2 %copy-start.6 = (bf16[1024,2048]{1,0:T(8,128)(2,1)S(1)}, bf16[1024,2048]{1,0:T(8,128)(2,1)}, u32[]{:S(2)}) copy-start(bf16[1024,2048]{1,0:T(8,128)(2,1)} %v_ref.7) | copy-start | bytes 12582916
  45.5 10.7 %copy-start.15 = (f32[2048]{0:T(1024)S(1)}, f32[2048]{0:T(1024)}, u32[]{:S(2)}) copy-start(f32[2048]{0:T(1024)} %param.14) | copy-start | bytes 24580
  56.2 2.2 %copy-start.1 = (bf16[1024,2048]{1,0:T(8,128)(2,1)S(1)}, bf16[1024,2048]{1,0:T(8,128)(2,1)}, u32[]{:S(2)}) copy-start(bf16[1024,2048]{1,0:T(8,128)(2,1)} %q_ref.5) | copy-start | bytes 12582916
  58.4 2.2 %copy-start.8 = (bf16[1024,2048]{1,0:T(8,128)(2,1)S(1)}, bf16[1024,2048]{1,0:T(8,128)(2,1)}, u32[]{:S(2)}) copy-start(bf16[1024,2048]{1,0:T(8,128)(2,1)} %refs_5_.1) | copy-start | bytes 12582916
  73.7 1.3 copy-start.18
  75.1 5.0 %collective-permute-start.2 = (f32[2,1024]{1,0:T(2,128)S(1)}, f32[2,1024]{1,0:T(2,128)S(1)}, u32[]{:S(2)}, u32[]{:S(2)}) collective-permute-start(f32[2,1024]{1,0:T(2,128)S(1)} %get-tuple-element.29.refs_0_), channel_id=1, source_target_pairs={{0,3},{1,0},{2,1},{3,2},{4,7},{5,4},{6,5},{7,6},{8,11},{9,8},{10,9... | collective-permute-start | bytes 24584 | tf_op jit(solution)/shard_map/ppermute | solution.py:361
  78.7 4.6 %collective-permute-start.1 = (f32[2,1024]{1,0:T(2,128)S(1)}, f32[2,1024]{1,0:T(2,128)S(1)}, u32[]{:S(2)}, u32[]{:S(2)}) collective-permute-start(f32[2,1024]{1,0:T(2,128)S(1)} %get-tuple-element.29.refs_0_), channel_id=1, source_target_pairs={{0,2},{1,3},{2,0},{3,1},{4,6},{5,7},{6,4},{7,5},{8,10},{9,11},{10,... | collective-permute-start | bytes 24584 | tf_op jit(solution)/shard_map/ppermute | solution.py:361
  78.7 5.4 %collective-permute-start = (f32[2,1024]{1,0:T(2,128)S(1)}, f32[2,1024]{1,0:T(2,128)S(1)}, u32[]{:S(2)}, u32[]{:S(2)}) collective-permute-start(f32[2,1024]{1,0:T(2,128)S(1)} %get-tuple-element.29.refs_0_), channel_id=1, source_target_pairs={{0,1},{1,2},{2,3},{3,0},{4,5},{5,6},{6,7},{7,4},{8,9},{9,10},{10,1... | collective-permute-start | bytes 24584 | tf_op jit(solution)/shard_map/ppermute | solution.py:361
  97.2 2.0 %copy-start.9 = (f32[16,4,128,128]{3,2,1,0:T(8,128)}, f32[16,4,128,128]{3,2,1,0:T(8,128)S(1)}, u32[]{:S(2)}) copy-start(f32[16,4,128,128]{3,2,1,0:T(8,128)S(1)} %get-tuple-element.39.bloc_ref) | copy-start | bytes 12582916
  99.1 2.0 %copy-start.17 = (bf16[1024,2048]{1,0:T(8,128)(2,1)}, bf16[1024,2048]{1,0:T(8,128)(2,1)S(1)}, u32[]{:S(2)}) copy-start(bf16[1024,2048]{1,0:T(8,128)(2,1)S(1)} %get-tuple-element.33.agrad_ref) | copy-start | bytes 12582916
  121.6 32.5 %all-to-all-start.3 = ((f32[8,2,128,128]{3,2,1,0:T(8,128)}), f32[8,2,128,128]{3,2,1,0:T(8,128)S(1)}, u32[]{:S(2)}, u32[]{:S(2)}) async-start(f32[8,2,128,128]{3,2,1,0:T(8,128)} %shard_map.125), calls=%async_computation.3 | async-start | bytes 2097152 | tf_op jit(solution)/shard_map/all_to_all | solution.py:396
  125.2 1.6 copy-start.19
  150.0 2.0 %copy-start.11 = (bf16[1024,2048]{1,0:T(8,128)(2,1)}, bf16[1024,2048]{1,0:T(8,128)(2,1)S(1)}, u32[]{:S(2)}) copy-start(bf16[1024,2048]{1,0:T(8,128)(2,1)S(1)} %get-tuple-element.37.dkin_ref) | copy-start | bytes 12582916
  152.1 2.0 %copy-start.13 = (bf16[1024,2048]{1,0:T(8,128)(2,1)}, bf16[1024,2048]{1,0:T(8,128)(2,1)S(1)}, u32[]{:S(2)}) copy-start(bf16[1024,2048]{1,0:T(8,128)(2,1)S(1)} %get-tuple-element.38.dvin_ref) | copy-start | bytes 12582916
  154.1 2.2 %copy-start.4 = (bf16[1024,2048]{1,0:T(8,128)(2,1)S(1)}, bf16[1024,2048]{1,0:T(8,128)(2,1)}, u32[]{:S(2)}) copy-start(bf16[1024,2048]{1,0:T(8,128)(2,1)} %k_ref.7) | copy-start | bytes 12582916
  156.3 2.2 %copy-start.7 = (bf16[1024,2048]{1,0:T(8,128)(2,1)S(1)}, bf16[1024,2048]{1,0:T(8,128)(2,1)}, u32[]{:S(2)}) copy-start(bf16[1024,2048]{1,0:T(8,128)(2,1)} %v_ref.7) | copy-start | bytes 12582916
  158.5 2.2 %copy-start.12 = (bf16[1024,2048]{1,0:T(8,128)(2,1)S(1)}, bf16[1024,2048]{1,0:T(8,128)(2,1)}, u32[]{:S(2)}) copy-start(bf16[1024,2048]{1,0:T(8,128)(2,1)} %copy-done.11) | copy-start | bytes 12582916
  (1 other events, 0.7 us)

commit v2 on v1

v2 whole, which is shorter than its diff:
```python
import functools

import jax
import jax.numpy as jnp
from jax import lax
from jax.experimental import pallas as pl
from jax.experimental.pallas import tpu as pltpu
from jax.sharding import PartitionSpec as P

HEAD_TOTAL = 64
HD = 128
CHUNK = 256
GROUP = 2
WINDOWS = 4
WIDTH = HEAD_TOTAL * HD

epsilon = 1e-06
LOG2E = 1.4426950408889634

F32 = jnp.float32
BF16 = jnp.bfloat16
MIB = 1024 * 1024
NT = ((1,), (1,))


def dot(a, b, dims=((1,), (0,))):
    return lax.dot_general(a, b, (dims, ((), ())), preferred_element_type=F32)


def column(row):
    return jnp.broadcast_to(row, (HD, row.shape[1])).T


def spread(cols, lane, width=HD):
    return jnp.broadcast_to(cols[:, lane : lane + 1], (cols.shape[0], width))


def turned(cols_ref, first):
    return pltpu.roll(cols_ref[...], (HD - first) % HD, 1)


def chunk_cumsum(x):
    lane = lax.broadcasted_iota(jnp.int32, x.shape, 1) % CHUNK
    shift = 1
    while shift < CHUNK:
        x = x + jnp.where(lane >= shift, pltpu.roll(x, shift, 1), 0.0)
        shift *= 2
    return x


def fill_masks(rrow_ref, mask_ref, transposed):
    for n in range(mask_ref.shape[0]):
        r_row = rrow_ref[0:1, n * CHUNK : (n + 1) * CHUNK]
        r_col = jnp.concatenate([column(r_row)] * (CHUNK // HD), axis=1)
        sub = lax.broadcasted_iota(jnp.int32, (CHUNK, CHUNK), 0)
        lane = lax.broadcasted_iota(jnp.int32, (CHUNK, CHUNK), 1)
        causal = (sub <= lane) if transposed else (lane <= sub)
        mask_ref[n] = jnp.where((r_col == r_row) & causal, 0.0, -jnp.inf)


def state_kernel(
    chunks, heads, lc_ref, doc_ref, k_ref, v_ref,
    crow_ref, enter_ref, leave_ref, rrow_ref, cols_ref, loc_ref, state_ref,
):
    step = pl.program_id(0)

    @pl.when(step == 0)
    def _():
        c = chunk_cumsum(lc_ref[...] * LOG2E)
        r = chunk_cumsum(jnp.broadcast_to(doc_ref[...].astype(F32), (8, doc_ref.shape[1])))
        crow_ref[...] = c
        rrow_ref[...] = r
        enter = jnp.where(r[0:1] == 0.0, jnp.exp2(c), 0.0)
        enter_ref[...] = enter
        spare = jnp.zeros((HD - 3 * heads, CHUNK), F32)
        for n in range(chunks):
            span = slice(n * CHUNK, (n + 1) * CHUNK)
            cn, rn = c[:, span], r[0:1, span]
            leave = jnp.where(rn == rn[:, -1:], jnp.exp2(cn[:, -1:] - cn), 0.0)
            leave_ref[:, span] = leave
            cols_ref[span, :] = jnp.concatenate([cn, enter[:, span], leave, spare], axis=0).T

    for g in range(GROUP):
        h = step * GROUP + g
        cols = slice(g * HD, (g + 1) * HD)
        state = None
        for n in range(chunks):
            span = slice(n * CHUNK, (n + 1) * CHUNK)
            keyed = (k_ref[span, cols].T.astype(F32) * leave_ref[pl.ds(h, 1), span]).astype(BF16)
            local = dot(keyed, v_ref[span, cols])
            loc_ref[g, n] = local
            passing = enter_ref[pl.ds(h, 1), span][:, CHUNK - 1 : CHUNK]
            state = local if state is None else passing * state + local
        state_ref[g] = state


def inside_kernel(
    chunks, first, rrow_ref, crow_ref, cols_ref, gain_ref, q_ref, k_ref, v_ref, gate_ref,
    grad_ref, *refs,
):
    out_ref, gnorm_ref, mask_ref = refs[-3:]
    step = pl.program_id(0)

    @pl.when(step == 0)
    def _():
        fill_masks(rrow_ref, mask_ref, False)

    cols_now = turned(cols_ref, first + step * GROUP)
    for g in range(GROUP):
        h = first + step * GROUP + g
        cols = slice(g * HD, (g + 1) * HD)
        for n in range(chunks):
            span = slice(n * CHUNK, (n + 1) * CHUNK)
            c_row = crow_ref[pl.ds(h, 1), span]
            c_col = spread(cols_now[span], g, CHUNK)
            weight = jnp.exp2(c_col - c_row + mask_ref[n])
            scores = dot(q_ref[span, cols], k_ref[span, cols], NT)
            probs = (scores * weight).astype(BF16)
            out_ref[span, cols] = dot(probs, v_ref[span, cols])
            sig = jax.nn.sigmoid(gate_ref[span, cols].astype(F32))
            gnorm = grad_ref[span, cols].astype(F32) * sig * gain_ref[0:1, cols]
            gnorm_ref[span, cols] = gnorm.astype(BF16)


def outside_kernel(
    chunks, heads, cols_ref, enter_ref, q_ref, gnorm_ref, inside_ref, loc_ref, in_ref,
    attn_ref, held_ref, sums_ref, sq_ref, inner_ref,
):
    step = pl.program_id(0)

    @pl.when(step == 0)
    def _():
        sq_ref[...] = jnp.zeros_like(sq_ref)
        inner_ref[...] = jnp.zeros_like(inner_ref)

    cols_now = turned(cols_ref, heads + step * GROUP)
    carries = [in_ref[g] for g in range(GROUP)]
    for n in range(chunks):
        span = slice(n * CHUNK, (n + 1) * CHUNK)
        squares = sq_ref[span, :]
        inners = inner_ref[span, :]
        for g in range(GROUP):
            h = step * GROUP + g
            cols = slice(g * HD, (g + 1) * HD)
            held = carries[g].astype(BF16)
            held_ref[g, n] = held
            enter = spread(cols_now[span], g)
            attn = inside_ref[span, cols] + enter * dot(q_ref[span, cols], held)
            attn_ref[span, cols] = attn
            squares = squares + attn * attn
            inners = inners + gnorm_ref[span, cols].astype(F32) * attn
            if n + 1 < chunks:
                passing = enter_ref[pl.ds(h, 1), span][:, CHUNK - 1 : CHUNK]
                carries[g] = passing * carries[g] + loc_ref[g, n]
        sq_ref[span, :] = squares
        inner_ref[span, :] = inners

    @pl.when(step == pl.num_programs(0) - 1)
    def _():
        sums_ref[0:1, :] = jnp.sum(sq_ref[...].T, axis=0, keepdims=True)
        sums_ref[1:2, :] = jnp.sum(inner_ref[...].T, axis=0, keepdims=True)


def token_scales(sums_refs):
    sums = sums_refs[0][...]
    for ref in sums_refs[1:]:
        sums = sums + ref[...]
    inverse = lax.rsqrt(sums[0:1] / WIDTH + epsilon)
    return inverse, inverse * inverse * inverse * sums[1:2] / WIDTH


def grad_kernel(chunks, parts, enter_ref, *refs):
    q_ref, gnorm_ref, attn_ref, agrad_ref, bloc_ref, back_ref, alpha_ref, beta_ref = refs[parts:]
    step = pl.program_id(0)

    @pl.when(step == 0)
    def _():
        inverse, slope = token_scales(refs[:parts])
        alpha_ref[...] = column(inverse)
        beta_ref[...] = column(slope)

    backs = [None] * GROUP
    for n in reversed(range(chunks)):
        span = slice(n * CHUNK, (n + 1) * CHUNK)
        alpha, beta = alpha_ref[span, :], beta_ref[span, :]
        for g in range(GROUP):
            h = step * GROUP + g
            cols = slice(g * HD, (g + 1) * HD)
            enter = enter_ref[pl.ds(h, 1), span]
            gnorm = gnorm_ref[span, cols].astype(F32)
            agrad = (alpha * gnorm - attn_ref[span, cols] * beta).astype(BF16)
            agrad_ref[span, cols] = agrad
            qkeyed = (q_ref[span, cols].T.astype(F32) * enter).astype(BF16)
            local = dot(qkeyed, agrad)
            bloc_ref[g, n] = local
            passing = enter[:, CHUNK - 1 : CHUNK]
            backs[g] = local if backs[g] is None else local + passing * backs[g]
    for g in range(GROUP):
        back_ref[g] = backs[g]


def gate_kernel(chunks, parts, gain_ref, *refs):
    gate_ref, grad_ref, attn_ref, gated_ref, ggate_ref, alpha_ref = refs[parts:]
    step = pl.program_id(0)

    @pl.when(step == 0)
    def _():
        inverse, _ = token_scales(refs[:parts])
        alpha_ref[...] = column(inverse)

    for n in range(chunks):
        span = slice(n * CHUNK, (n + 1) * CHUNK)
        alpha = alpha_ref[span, :]
        for g in range(GROUP):
            cols = slice(g * HD, (g + 1) * HD)
            sig = jax.nn.sigmoid(gate_ref[span, cols].astype(F32))
            gated = attn_ref[span, cols] * alpha * gain_ref[0:1, cols] * sig
            gated_ref[span, cols] = gated.astype(BF16)
            ggate = grad_ref[span, cols].astype(F32) * gated * (1.0 - sig)
            ggate_ref[span, cols] = ggate.astype(BF16)


def inner_grad_kernel(
    chunks, first, rrow_ref, crow_ref, enter_ref, cols_ref, q_ref, k_ref, v_ref, agrad_ref,
    held_ref, *refs,
):
    dq_ref, dk_ref, dv_ref, mask_ref = refs[-4:]
    step = pl.program_id(0)

    @pl.when(step == 0)
    def _():
        fill_masks(rrow_ref, mask_ref, True)

    cols_now = turned(cols_ref, first + step * GROUP)
    for g in range(GROUP):
        h = first + step * GROUP + g
        cols = slice(g * HD, (g + 1) * HD)
        for n in range(chunks):
            span = slice(n * CHUNK, (n + 1) * CHUNK)
            c_row = crow_ref[pl.ds(h, 1), span]
            c_col = spread(cols_now[span], g, CHUNK)
            q, k = q_ref[span, cols], k_ref[span, cols]
            v, agrad = v_ref[span, cols], agrad_ref[span, cols]
            weight = jnp.exp2(c_row - c_col + mask_ref[n])
            probs = (dot(k, q, NT) * weight).astype(BF16)
            dv_ref[span, cols] = dot(probs, agrad).astype(BF16)
            both = dot(jnp.concatenate([v, held_ref[g, n]], axis=0), agrad, NT)
            dscore = (both[:CHUNK] * weight).astype(BF16)
            dk_ref[span, cols] = dot(dscore, q).astype(BF16)
            dq = dot(k.T, dscore) + enter_ref[pl.ds(h, 1), span] * both[CHUNK:]
            dq_ref[span, cols] = dq.astype(BF16).T


def outer_grad_kernel(
    chunks, heads, cols_ref, enter_ref, k_ref, v_ref, dkin_ref, dvin_ref, bloc_ref, out_ref,
    dk_ref, dv_ref,
):
    step = pl.program_id(0)
    cols_now = turned(cols_ref, 2 * heads + step * GROUP)
    for g in range(GROUP):
        h = step * GROUP + g
        cols = slice(g * HD, (g + 1) * HD)
        carry = out_ref[g]
        for n in reversed(range(chunks)):
            span = slice(n * CHUNK, (n + 1) * CHUNK)
            leave = spread(cols_now[span], g)
            back = carry.astype(BF16)
            dk = dkin_ref[span, cols].astype(F32) + leave * dot(v_ref[span, cols], back, NT)
            dv = dvin_ref[span, cols].astype(F32) + leave * dot(k_ref[span, cols], back)
            dk_ref[span, cols] = dk.astype(BF16)
            dv_ref[span, cols] = dv.astype(BF16)
            if n > 0:
                passing = enter_ref[pl.ds(h, 1), span][:, CHUNK - 1 : CHUNK]
                carry = bloc_ref[g, n] + passing * carry


def call(kernel, grid, ins, outs, scratch=(), aliases=None, flops=0, moved=0, exps=0):
    arrays, shapes = [], []
    for x, _ in ins:
        large = x.size * x.dtype.itemsize >= MIB
        arrays.append(pltpu.with_memory_space_constraint(x, pltpu.HBM) if large else x)
    for dims, dtype, _ in outs:
        large = jnp.dtype(dtype).itemsize * functools.reduce(lambda a, b: a * b, dims) >= MIB
        shapes.append(pltpu.HBM(dims, dtype) if large else jax.ShapeDtypeStruct(dims, dtype))
    return pl.pallas_call(
        kernel,
        grid=grid,
        in_specs=[spec for _, spec in ins],
        out_specs=[spec for _, _, spec in outs],
        out_shape=shapes,
        scratch_shapes=list(scratch),
        input_output_aliases=aliases or {},
        compiler_params=pltpu.CompilerParams(
            dimension_semantics=("arbitrary",) * len(grid), vmem_limit_bytes=40 * MIB
        ),
        cost_estimate=pl.CostEstimate(flops=flops, bytes_accessed=moved, transcendentals=exps),
    )(*arrays)


def after(x, *others):
    return lax.optimization_barrier((x, *others))[0]


def swap(x, bit, devices):
    return lax.ppermute(x, "seq", [(i, i ^ (1 << bit)) for i in range(devices)])


def cube_scan(state, passes, index, fill):
    heads = state.shape[0]
    half, quarter = heads // 2, heads // 4
    core, x, y = index % 2, (index // 2) % 2, index // 4
    chip = index // 2
    factor = lambda rows: rows[:, None, None]

    other = swap(state, 0, 8)
    other = after(other, fill(0, state))
    early = jnp.where(core == 0, state, other)
    late = jnp.where(core == 0, other, state)
    even = lax.dynamic_index_in_dim(passes, 2 * chip, 0, False)
    odd = lax.dynamic_index_in_dim(passes, 2 * chip + 1, 0, False)
    mine = lambda a, axis: lax.dynamic_slice_in_dim(a, core * half, half, axis)
    total = factor(mine(odd, 0)) * mine(early, 0) + mine(late, 0)
    chip_pass = mine(passes[0::2] * passes[1::2], 1)
    to_x, to_y = total[:quarter], total[quarter:]
    pass_x, pass_y = chip_pass[:, :quarter], chip_pass[:, quarter:]

    from_x, from_y = swap(to_x, 1, 8), swap(to_y, 2, 8)
    from_x, from_y = lax.optimization_barrier((from_x, from_y, fill(1, total)))[:2]
    left = jnp.where(x == 0, to_x, from_x)
    right = jnp.where(x == 0, from_x, to_x)
    row = factor(jnp.where(y == 0, pass_x[1], pass_x[3])) * left + right
    through = factor(pass_y[2]) * (factor(pass_y[1]) * from_y) + to_y
    sent = jnp.where(y == 0, to_y, jnp.where(x == 0, through, from_y))

    row_in, sent_in = swap(row, 2, 8), swap(sent, 1, 8)
    row_in, sent_in = lax.optimization_barrier((row_in, sent_in, fill(2, sent)))[:2]
    lower = jnp.where(x == 0, row_in, factor(pass_x[2]) * row_in + from_x)
    upper = jnp.where(x == 0, 0.0, from_x)
    in_x = jnp.where(y == 0, upper, lower)
    more = factor(jnp.where(x == 0, pass_y[1], pass_y[2])) * from_y
    in_y = jnp.where(y == 0, jnp.where(x == 0, 0.0, sent_in), more + sent_in)
    ahead = jnp.concatenate([in_x, in_y], axis=0)

    beside = swap(ahead, 0, 8)
    beside = after(beside, fill(3, ahead))
    low = jnp.where(core == 0, ahead, beside)
    high = jnp.where(core == 0, beside, ahead)
    entering = jnp.concatenate([low, high], axis=0)
    return jnp.where(core == 0, entering, factor(even) * entering + early)


def doubling_scan(state, passes, index, fill, reverse):
    devices = passes.shape[0]
    route = lambda hop: [
        (i, i - hop if reverse else i + hop)
        for i in range(devices)
        if 0 <= (i - hop if reverse else i + hop) < devices
    ]
    for window in range(WINDOWS):
        state = after(state, fill(window, state))
    hop = 1
    while hop < devices:
        factor = lax.dynamic_index_in_dim(passes, index, 0, False)
        state = factor[:, None, None] * lax.ppermute(state, "seq", route(hop)) + state
        before = jnp.concatenate([jnp.zeros_like(passes[:hop]), passes[:-hop]], axis=0)
        passes = passes * before
        hop *= 2
    return lax.ppermute(state, "seq", route(1))


def scan_devices(state, passes, fill, reverse):
    devices = passes.shape[0]
    index = lax.axis_index("seq")
    if reverse:
        passes = passes[::-1]
        index = devices - 1 - index
    if devices == 8 and state.shape[0] % 4 == 0:
        return cube_scan(state, passes, index, fill)
    return doubling_scan(state, passes, index, fill, reverse)


def body(queries, key_rows, value_rows, log_decay, doc_start, gate_input, norm_gain, out_grad):
    rows, cols = queries.shape
    heads = cols // HD
    chunks = rows // CHUNK
    parts = lax.axis_size("head")
    grid = (heads // GROUP,)
    share = heads // WINDOWS
    big = rows * cols * 2
    tile = 2 * rows * CHUNK * cols
    small = 2 * rows * HD * cols

    whole = lambda *dims: pl.BlockSpec(dims, lambda i: (0,) * len(dims))

    def wide(base=0):
        return pl.BlockSpec((rows, GROUP * HD), lambda i: (0, i + base // GROUP))

    def loc(base=0):
        return pl.BlockSpec((GROUP, chunks, HD, HD), lambda i: (i + base // GROUP, 0, 0, 0))

    state_spec = pl.BlockSpec((GROUP, HD, HD), lambda i: (i, 0, 0))
    gain_spec = lambda base=0: pl.BlockSpec((1, GROUP * HD), lambda i: (0, i + base // GROUP))
    row_spec = whole(heads, rows)
    rrow_spec = whole(8, rows)
    cols_spec = whole(rows, HD)
    sums_spec = whole(2, rows)
    anywhere = pl.BlockSpec(memory_space=pl.ANY)
    mask = pltpu.VMEM((chunks, CHUNK, CHUNK), F32)
    tall = pltpu.VMEM((rows, HD), F32)

    doc_row = doc_start.reshape(1, rows)
    gain_row = norm_gain.reshape(1, cols)
    dev_pass = jnp.where(jnp.any(doc_start != 0), 0.0, jnp.exp(jnp.sum(log_decay, axis=1)))
    passes = lax.all_gather(dev_pass, "seq")

    loc_out = ((heads, chunks, HD, HD), F32, loc())
    state_out = ((heads, HD, HD), F32, state_spec)
    wide_out = ((rows, cols), BF16, wide())
    row_out = ((heads, rows), F32, row_spec)

    crow, enter, leave, rrow, columns, local, state = call(
        functools.partial(state_kernel, chunks, heads),
        grid,
        [(log_decay, row_spec), (doc_row, whole(1, rows)), (key_rows, wide()), (value_rows, wide())],
        [
            row_out, row_out, row_out, ((8, rows), F32, rrow_spec),
            ((rows, HD), F32, cols_spec), loc_out, state_out,
        ],
        flops=small, moved=2 * big + 6 * MIB,
    )

    made = []

    def fill_forward(window, tie):
        base = window * share
        spec = wide(base)
        ins = [
            (after(rrow, tie), rrow_spec), (crow, row_spec), (columns, cols_spec),
            (gain_row, gain_spec(base)), (queries, spec), (key_rows, spec), (value_rows, spec),
            (gate_input, spec), (out_grad, spec),
        ]
        aliases = {}
        if made:
            aliases = {len(ins): 0, len(ins) + 1: 1}
            ins += [(x, anywhere) for x in made]
        made[:] = call(
            functools.partial(inside_kernel, chunks, base),
            (share // GROUP,),
            ins,
            [((rows, cols), F32, spec), ((rows, cols), BF16, spec)],
            [mask],
            aliases,
            flops=2 * tile // WINDOWS, moved=8 * big // WINDOWS,
            exps=rows * (CHUNK + HD) * heads // WINDOWS,
        )
        return made[1]

    incoming = scan_devices(state, passes, fill_forward, False)
    inside, gnorm = made

    attn, held, sums = call(
        functools.partial(outside_kernel, chunks, heads),
        grid,
        [
            (columns, cols_spec), (enter, row_spec), (queries, wide()), (gnorm, wide()),
            (inside, wide()), (local, loc()), (incoming, state_spec),
        ],
        [
            ((rows, cols), F32, wide()), ((heads, chunks, HD, HD), BF16, loc()),
            ((2, rows), F32, sums_spec),
        ],
        [tall, tall],
        flops=small, moved=6 * big + 7 * MIB,
    )

    all_sums = [(sums, sums_spec)]
    for hop in range(1, parts):
        route = [(i, (i + hop) % parts) for i in range(parts)]
        all_sums.append((lax.ppermute(sums, "head", route), sums_spec))

    agrad, bloc, back = call(
        functools.partial(grad_kernel, chunks, parts),
        grid,
        [(enter, row_spec)] + all_sums + [(queries, wide()), (gnorm, wide()), (attn, wide())],
        [wide_out, loc_out, state_out],
        [tall, tall],
        flops=small, moved=5 * big + 5 * MIB,
    )

    grads = []
    gates = []

    def fill_backward(window, tie):
        base = window * share
        spec = wide(base)
        ins = [
            (after(rrow, tie), rrow_spec), (crow, row_spec), (enter, row_spec),
            (columns, cols_spec), (queries, spec), (key_rows, spec), (value_rows, spec),
            (agrad, spec), (held, loc(base)),
        ]
        aliases = {}
        if grads:
            aliases = {len(ins): 0, len(ins) + 1: 1, len(ins) + 2: 2}
            ins += [(x, anywhere) for x in grads]
        grads[:] = call(
            functools.partial(inner_grad_kernel, chunks, base),
            (share // GROUP,),
            ins,
            [((rows, cols), BF16, spec)] * 3,
            [mask],
            aliases,
            flops=(5 * tile + small) // WINDOWS, moved=8 * big // WINDOWS,
            exps=rows * CHUNK * heads // WINDOWS,
        )
        if window != 1:
            return grads[2]
        gates[:] = call(
            functools.partial(gate_kernel, chunks, parts),
            grid,
            [(after(gain_row, grads[2]), gain_spec())] + all_sums
            + [(gate_input, wide()), (out_grad, wide()), (attn, wide())],
            [wide_out, wide_out],
            [tall],
            flops=20 * rows * cols, moved=6 * big, exps=rows * cols,
        )
        return gates[1]

    outgoing = scan_devices(back, passes, fill_backward, True)
    dq, dk_inner, dv_inner = grads

    dk, dv = call(
        functools.partial(outer_grad_kernel, chunks, heads),
        grid,
        [
            (columns, cols_spec), (enter, row_spec), (key_rows, wide()), (value_rows, wide()),
            (dk_inner, wide()), (dv_inner, wide()), (bloc, loc()), (outgoing, state_spec),
        ],
        [wide_out, wide_out],
        flops=2 * small, moved=6 * big + 5 * MIB,
    )
    return (*gates, dq, dk, dv)


def solution(mesh):
    in_specs = (
        P("seq", "head"),
        P("seq", "head"),
        P("seq", "head"),
        P("head", "seq"),
        P("seq"),
        P("seq", "head"),
        P("head"),
        P("seq", "head"),
    )
    out_specs = (P("seq", "head"),) * 5
    return jax.shard_map(body, mesh=mesh, in_specs=in_specs, out_specs=out_specs, check_vma=False)
```

time: 172 us -> 157 us (0.913)
  Pallas kernels: 77.4 us -> 112 us
  local copies, waits for them, and re-layouts: 36.3 us -> 2.71 us
  blocking collectives: 40.3 us -> 15.3 us
  other arithmetic: 0 us -> 5.63 us
    all_to_all x2 -> x0, blocking collectives: 40.3 us -> none  [the longest x1 21 us: body(): ext = lax.all_to_all(sext.reshape(devices, own, piece + 8, HD), 'seq', 0, 0)]
    pallas_call x8 -> x13, Pallas kernels: 77.4 us -> 112 us  [call(): pl.pallas_call(kernel, grid=grid, in_specs=[spec for _, spec in ins], out...]
    unnamed x40 -> x18, local copies, waits for them, and re-layouts: 36.3 us -> 2.13 us
    unnamed x0 -> x1, blocking collectives: none -> 15.3 us
    ppermute x3 -> x15, starting transfers between devices: 4.64 us -> 12.8 us  [the longest x12 8.18 us: swap(): return lax.ppermute(x, 'seq', [(i, i ^ 1 << bit) for i in range(devices)])]
    all_to_all x2 -> x0, starting transfers between devices: 7.12 us -> none  [the longest x1 3.56 us: body(): incoming = lax.all_to_all(before, 'seq', 0, 0).reshape(heads, HD, HD)]
    select_n x0 -> x13, other arithmetic: none -> 3.64 us  [the longest x2 2.37 us: cube_scan(): return jnp.where(core == 0, entering, factor(even) * entering + early)]
    ppermute x3 -> x15, waiting for transfers between devices: 4.41 us -> 5.74 us  [the longest x3 4.44 us: body(): all_sums.append((lax.ppermute(sums, 'head', route), sums_spec))]
  transfers between devices with their start and end apart: 5 -> 15, of which waited for: 3 -> 6; matrix products, arithmetic and copies ran while one was open for 0% -> 2% of each run, Pallas kernels for 20% -> 39%
where the time goes in v2:
time: 157 us; the launch traced here: 156 us
  Pallas kernels  112 us (71%)
  blocking collectives  15.3 us (10%)
  starting transfers between devices  12.8 us (8%)
  waiting for transfers between devices  5.74 us (4%)
  other arithmetic  5.63 us (4%)
  local copies, waits for them, and re-layouts  2.71 us (2%)
  between operations  1.58 us (1%)
    pallas_call x13, Pallas kernels, call(): pl.pallas_call(kernel, grid=grid, in_specs=[spec for _, spec in ins], out...  112 us
    unnamed x1, blocking collectives  15.3 us
    ppermute x12, starting transfers between devices, swap(): return lax.ppermute(x, 'seq', [(i, i ^ 1 << bit) for i in range(devices)])  8.18 us
    ppermute x3, starting transfers between devices, body(): all_sums.append((lax.ppermute(sums, 'head', route), sums_spec))  4.62 us
    ppermute x3, waiting for transfers between devices, body(): all_sums.append((lax.ppermute(sums, 'head', route), sums_spec))  4.44 us
  transfers between devices with their start and end apart: 15, of which 6 were waited for; matrix products, arithmetic and copies ran while one was open for 2% of the time, Pallas kernels for 39%

profile of v2, /device:TPU:0, one launch (start us, length us, event | category | flops | bytes accessed | tf_op | source)
XLA Modules:
  0.0 155.8 jit_solution(11495981400621442095)
XLA Ops:
  2.2 9.8 %shard_map.119 = (f32[16,1024]{1,0:T(8,128)S(1)}, f32[16,1024]{1,0:T(8,128)S(1)}, f32[16,1024]{1,0:T(8,128)}, f32[8,1024]{1,0:T(8,128)S(1)}, f32[1024,128]{1,0:T...) custom-call(f32[16,1024]{1,0:T(8,128)S(1)} %copy-done, s32[1,1024]{1,0:T(1,128)S(1)} %bitcast.40, ...), custom_call_target="tpu_custom_call" | custom-call | flops 536870912 | bytes 14680064 | tf_op jit(solution)/shard_map/pallas_call | solution.py:285
  15.2 15.3 %all-reduce = f32[128]{0:T(128)S(1)} all-reduce(f32[128]{0:T(128)S(1)} %fusion.2), channel_id=2, replica_groups=mesh['seq'=8,'head'=4] {'seq'}, use_global_device_ids=true, to_apply=%add | all-reduce | flops 128 | bytes 1024
  30.7 5.6 %shard_map.120 = (f32[1024,2048]{1,0:T(8,128)}, bf16[1024,2048]{1,0:T(8,128)(2,1)}) custom-call(f32[8,1024]{1,0:T(8,128)S(1)} %get-tuple-element.109.rrow_ref, f32[16,1024]{1,0:T(8,128)S(1)} %get-tuple-element.67.crow_ref, f32[1024,128]{1,0:T(8,128)S(1)} %get-tuple-element.64.cols_ref, f32[1,2048]{1,0:T(1,128)S(1)} %bitcast.35, bf16[1024,2048]{1,0:T(8,128)(2,1)} %q_ref.17, ...), custom_call_target="tpu_custom_call" | custom-call | flops 536870912 | bytes 8388608 | tf_op jit(solution)/shard_map/pallas_call | solution.py:285
  37.5 5.5 %shard_map.121 = (f32[1024,2048]{1,0:T(8,128)}, bf16[1024,2048]{1,0:T(8,128)(2,1)}) custom-call(f32[8,1024]{1,0:T(8,128)S(1)} %get-tuple-element.109.rrow_ref, f32[16,1024]{1,0:T(8,128)S(1)} %get-tuple-element.67.crow_ref, f32[1024,128]{1,0:T(8,128)S(1)} %get-tuple-element.64.cols_ref, ...), custom_call_target="tpu_custom_call", output_to_operand_aliasing={{0}: (9, {}), {1}: (10, {})} | custom-call | flops 536870912 | bytes 8388608 | tf_op jit(solution)/shard_map/pallas_call | solution.py:285
  43.9 1.6 %collective-permute-start.3 = (f32[4,128,128]{2,1,0:T(8,128)S(1)}, f32[4,128,128]{2,1,0:T(8,128)S(1)}, u32[]{:S(2)}, u32[]{:S(2)}) collective-permute-start(f32[4,128,128]{2,1,0:T(8,128)S(1)} %get-tuple-element.128), channel_id=1, source_target_pairs={{0,16},{4,20},{8,24},{12,28},{16,0},{20,4},{24,8},{28,12},{1,17},{... | collective-permute-start | bytes 786440 | tf_op jit(solution)/shard_map/ppermute | solution.py:305
  45.5 1.2 collective-permute-start.4
  46.8 5.5 %shard_map.122 = (f32[1024,2048]{1,0:T(8,128)}, bf16[1024,2048]{1,0:T(8,128)(2,1)}) custom-call(f32[8,1024]{1,0:T(8,128)S(1)} %get-tuple-element.109.rrow_ref, f32[16,1024]{1,0:T(8,128)S(1)} %get-tuple-element.67.crow_ref, f32[1024,128]{1,0:T(8,128)S(1)} %get-tuple-element.64.cols_ref, ...), custom_call_target="tpu_custom_call", output_to_operand_aliasing={{0}: (9, {}), {1}: (10, {})} | custom-call | flops 536870912 | bytes 8388608 | tf_op jit(solution)/shard_map/pallas_call | solution.py:285
  52.6 5.5 %shard_map.123 = (f32[1024,2048]{1,0:T(8,128)}, bf16[1024,2048]{1,0:T(8,128)(2,1)}) custom-call(f32[8,1024]{1,0:T(8,128)S(1)} %get-tuple-element.109.rrow_ref, f32[16,1024]{1,0:T(8,128)S(1)} %get-tuple-element.67.crow_ref, f32[1024,128]{1,0:T(8,128)S(1)} %get-tuple-element.64.cols_ref, ...), custom_call_target="tpu_custom_call", output_to_operand_aliasing={{0}: (9, {}), {1}: (10, {})} | custom-call | flops 536870912 | bytes 8388608 | tf_op jit(solution)/shard_map/pallas_call | solution.py:285
  58.2 1.2 add_select_fusion.1.in_ref
  59.4 14.9 %shard_map.124 = (f32[1024,2048]{1,0:T(8,128)}, bf16[16,4,128,128]{3,2,1,0:T(8,128)(2,1)}, f32[2,1024]{1,0:T(2,128)S(1)}) custom-call(f32[1024,128]{1,0:T(8,128)S(1)} %get-tuple-element.64.cols_ref, f32[16,1024]{1,0:T(8,128)S(1)} %get-tuple-element.63.enter_ref, bf16[1024,2048]{1,0:T(8,128)(2,1)} %q_ref.17, ...), custom_call_target="tpu_custom_call" | custom-call | flops 536870912 | bytes 32505856 | tf_op jit(solution)/shard_map/pallas_call | solution.py:285
  74.3 3.6 %collective-permute-start.8 = (f32[2,1024]{1,0:T(2,128)S(1)}, f32[2,1024]{1,0:T(2,128)S(1)}, u32[]{:S(2)}, u32[]{:S(2)}) collective-permute-start(f32[2,1024]{1,0:T(2,128)S(1)} %get-tuple-element.86.refs_0_), channel_id=1, source_target_pairs={{0,3},{1,0},{2,1},{3,2},{4,7},{5,4},{6,5},{7,6},{8,11},{9,8},{10,9... | collective-permute-start | bytes 24584 | tf_op jit(solution)/shard_map/ppermute | solution.py:479
  77.9 1.0 collective-permute-start.6
  79.3 3.2 %collective-permute-done.7.refs_2_ = f32[2,1024]{1,0:T(2,128)S(1)} collective-permute-done((f32[2,1024]{1,0:T(2,128)S(1)}, f32[2,1024]{1,0:T(2,128)S(1)}, u32[]{:S(2)}, u32[]{:S(2)}) %collective-permute-start.7) | collective-permute-done | bytes 8224 | tf_op jit(solution)/shard_map/ppermute | solution.py:479
  82.5 0.9 collective-permute-done.6.refs_1_
  83.4 12.1 %shard_map.125 = (bf16[1024,2048]{1,0:T(8,128)(2,1)}, f32[16,4,128,128]{3,2,1,0:T(8,128)}, f32[16,128,128]{2,1,0:T(8,128)}) custom-call(f32[16,1024]{1,0:T(8,128)S(1)} %get-tuple-element.63.enter_ref, f32[2,1024]{1,0:T(2,128)S(1)} %get-tuple-element.86.refs_0_, f32[2,1024]{1,0:T(2,128)S(1)} %collective-permute-done.6.refs_1_, ...), custom_call_target="tpu_custom_call" | custom-call | flops 536870912 | bytes 26214400 | tf_op jit(solution)/shard_map/pallas_call | solution.py:285
  95.8 6.7 %shard_map.126 = (bf16[1024,2048]{1,0:T(8,128)(2,1)}, bf16[1024,2048]{1,0:T(8,128)(2,1)}, bf16[1024,2048]{1,0:T(8,128)(2,1)}) custom-call(f32[8,1024]{1,0:T(8,128)S(1)} %get-tuple-element.109.rrow_ref, f32[16,1024]{1,0:T(8,128)S(1)} %get-tuple-element.67.crow_ref, f32[16,1024]{1,0:T(8,128)S(1)} %get-tuple-element.63.enter_ref, ...), custom_call_target="tpu_custom_call" | custom-call | flops 1476395008 | bytes 8388608 | tf_op jit(solution)/shard_map/pallas_call | solution.py:285
  103.7 1.1 collective-permute-start.10
  104.8 6.6 %shard_map.127 = (bf16[1024,2048]{1,0:T(8,128)(2,1)}, bf16[1024,2048]{1,0:T(8,128)(2,1)}, bf16[1024,2048]{1,0:T(8,128)(2,1)}) custom-call(f32[8,1024]{1,0:T(8,128)S(1)} %get-tuple-element.109.rrow_ref, f32[16,1024]{1,0:T(8,128)S(1)} %get-tuple-element.67.crow_ref, ...), custom_call_target="tpu_custom_call", output_to_operand_aliasing={{0}: (9, {}), {1}: (10, {}), {2}: (11, {})} | custom-call | flops 1476395008 | bytes 8388608 | tf_op jit(solution)/shard_map/pallas_call | solution.py:285
  111.5 12.2 %shard_map.128 = (bf16[1024,2048]{1,0:T(8,128)(2,1)}, bf16[1024,2048]{1,0:T(8,128)(2,1)}) custom-call(f32[1,2048]{1,0:T(1,128)S(1)} %bitcast.39, f32[2,1024]{1,0:T(2,128)S(1)} %get-tuple-element.86.refs_0_, f32[2,1024]{1,0:T(2,128)S(1)} %collective-permute-done.6.refs_1_, f32[2,1024]{1,0:T(2,128)S(1)} %collective-permute-done.7.refs_2_, ...), custom_call_target="tpu_custom_call" | custom-call | flops 41943040 | bytes 25165824 | tf_op jit(solution)/shard_map/pallas_call | solution.py:285
  123.9 1.6 %collective-permute-start.12 = (f32[4,128,128]{2,1,0:T(8,128)S(1)}, f32[4,128,128]{2,1,0:T(8,128)S(1)}, u32[]{:S(2)}, u32[]{:S(2)}) collective-permute-start(f32[4,128,128]{2,1,0:T(8,128)S(1)} %get-tuple-element.124), channel_id=1, source_target_pairs={{0,16},{4,20},{8,24},{12,28},{16,0},{20,4},{24,8},{28,12},{1,17},{... | collective-permute-start | bytes 786440 | tf_op jit(solution)/shard_map/ppermute | solution.py:305
  126.2 6.6 %shard_map.129 = (bf16[1024,2048]{1,0:T(8,128)(2,1)}, bf16[1024,2048]{1,0:T(8,128)(2,1)}, bf16[1024,2048]{1,0:T(8,128)(2,1)}) custom-call(f32[8,1024]{1,0:T(8,128)S(1)} %get-tuple-element.109.rrow_ref, f32[16,1024]{1,0:T(8,128)S(1)} %get-tuple-element.67.crow_ref, ...), custom_call_target="tpu_custom_call", output_to_operand_aliasing={{0}: (9, {}), {1}: (10, {}), {2}: (11, {})} | custom-call | flops 1476395008 | bytes 8388608 | tf_op jit(solution)/shard_map/pallas_call | solution.py:285
  133.7 6.7 %shard_map.130 = (bf16[1024,2048]{1,0:T(8,128)(2,1)}, bf16[1024,2048]{1,0:T(8,128)(2,1)}, bf16[1024,2048]{1,0:T(8,128)(2,1)}) custom-call(f32[8,1024]{1,0:T(8,128)S(1)} %get-tuple-element.109.rrow_ref, f32[16,1024]{1,0:T(8,128)S(1)} %get-tuple-element.67.crow_ref, ...), custom_call_target="tpu_custom_call", output_to_operand_aliasing={{0}: (9, {}), {1}: (10, {}), {2}: (11, {})} | custom-call | flops 1476395008 | bytes 8388608 | tf_op jit(solution)/shard_map/pallas_call | solution.py:285
  140.5 1.2 add_select_fusion.out_ref
  141.7 14.1 %shard_map.131 = (bf16[1024,2048]{1,0:T(8,128)(2,1)}, bf16[1024,2048]{1,0:T(8,128)(2,1)}) custom-call(f32[1024,128]{1,0:T(8,128)S(1)} %get-tuple-element.64.cols_ref, f32[16,1024]{1,0:T(8,128)S(1)} %get-tuple-element.63.enter_ref, bf16[1024,2048]{1,0:T(8,128)(2,1)} %k_ref.19, bf16[1024,2048]{1,0:T(8,128)(2,1)} %v_ref.19, ...), custom_call_target="tpu_custom_call" | custom-call | flops 1073741824 | bytes 30408704 | tf_op jit(solution)/shard_map/pallas_call | solution.py:285
  (77 shorter events, 10.3 us)
Async XLA Ops:
  0.6 0.8 copy-start
  1.5 0.7 copy-start.3
  2.2 10.3 %copy-start.1 = (f32[16,1024]{1,0:T(8,128)S(1)}, f32[16,1024]{1,0:T(8,128)}, u32[]{:S(2)}) copy-start(f32[16,1024]{1,0:T(8,128)} %lc_ref.1) | copy-start | bytes 196612
  2.2 10.4 %copy-start.7 = (u32[32]{0:T(128)S(1)}, u32[32]{0:T(128)}, u32[]{:S(2)}) copy-start(u32[32]{0:T(128)} %constant.120) | copy-start | bytes 388
  2.2 11.7 %copy-start.4 = (s32[1024]{0:T(1024)S(1)}, s32[1024]{0:T(1024)}, u32[]{:S(2)}) copy-start(s32[1024]{0:T(1024)} %param.12) | copy-start | bytes 12292
  2.2 28.6 %copy-start.2 = (f32[2048]{0:T(1024)S(1)}, f32[2048]{0:T(1024)}, u32[]{:S(2)}) copy-start(f32[2048]{0:T(1024)} %param.14) | copy-start | bytes 24580
  12.0 24.5 %collective-permute-start = (f32[16,128,128]{2,1,0:T(8,128)}, f32[16,128,128]{2,1,0:T(8,128)S(1)}, u32[]{:S(2)}, u32[]{:S(2)}) collective-permute-start(f32[16,128,128]{2,1,0:T(8,128)} %get-tuple-element.65), channel_id=1, source_target_pairs={{0,4},{4,0},{8,12},{12,8},{16,20},{20,16},{24,28},{28,24},{1,5},{5... | collective-permute-start | bytes 3145736 | tf_op jit(solution)/shard_map/ppermute | solution.py:305
  30.7 5.8 %copy-start.5 = (f32[16,128,128]{2,1,0:T(8,128)S(1)}, f32[16,128,128]{2,1,0:T(8,128)}, u32[]{:S(2)}) copy-start(f32[16,128,128]{2,1,0:T(8,128)} %get-tuple-element.65) | copy-start | bytes 3145732
  36.8 6.4 %collective-permute-start.2 = (f32[4,128,128]{2,1,0:T(8,128)S(1)}, f32[4,128,128]{2,1,0:T(8,128)S(1)}, u32[]{:S(2)}, u32[]{:S(2)}) collective-permute-start(f32[4,128,128]{2,1,0:T(8,128)S(1)} %get-tuple-element.129), channel_id=1, source_target_pairs={{0,16},{4,20},{8,24},{12,28},{16,0},{20,4},{24,8},{28,12},{1,17},{... | collective-permute-start | bytes 786440 | tf_op jit(solution)/shard_map/ppermute | solution.py:305
  37.4 6.4 %collective-permute-start.1 = (f32[4,128,128]{2,1,0:T(8,128)S(1)}, f32[4,128,128]{2,1,0:T(8,128)S(1)}, u32[]{:S(2)}, u32[]{:S(2)}) collective-permute-start(f32[4,128,128]{2,1,0:T(8,128)S(1)} %get-tuple-element.130), channel_id=1, source_target_pairs={{0,8},{4,12},{8,0},{12,4},{16,24},{20,28},{24,16},{28,20},{1,9},{5... | collective-permute-start | bytes 786440 | tf_op jit(solution)/shard_map/ppermute | solution.py:305
  43.9 8.4 %collective-permute-start.3 = (f32[4,128,128]{2,1,0:T(8,128)S(1)}, f32[4,128,128]{2,1,0:T(8,128)S(1)}, u32[]{:S(2)}, u32[]{:S(2)}) collective-permute-start(f32[4,128,128]{2,1,0:T(8,128)S(1)} %get-tuple-element.128), channel_id=1, source_target_pairs={{0,16},{4,20},{8,24},{12,28},{16,0},{20,4},{24,8},{28,12},{1,17},{... | collective-permute-start | bytes 786440 | tf_op jit(solution)/shard_map/ppermute | solution.py:305
  45.5 6.8 %collective-permute-start.4 = (f32[4,128,128]{2,1,0:T(8,128)S(1)}, f32[4,128,128]{2,1,0:T(8,128)S(1)}, u32[]{:S(2)}, u32[]{:S(2)}) collective-permute-start(f32[4,128,128]{2,1,0:T(8,128)S(1)} %get-tuple-element.127), channel_id=1, source_target_pairs={{0,8},{4,12},{8,0},{12,4},{16,24},{20,28},{24,16},{28,20},{1,9},{5... | collective-permute-start | bytes 786440 | tf_op jit(solution)/shard_map/ppermute | solution.py:305
  52.5 5.6 %collective-permute-start.5 = (f32[8,128,128]{2,1,0:T(8,128)S(1)}, f32[8,128,128]{2,1,0:T(8,128)S(1)}, u32[]{:S(2)}, u32[]{:S(2)}) collective-permute-start(f32[8,128,128]{2,1,0:T(8,128)S(1)} %pad_maximum_fusion.2), channel_id=1, source_target_pairs={{0,4},{4,0},{8,12},{12,8},{16,20},{20,16},{24,28},{28,24},{1,5},{5... | collective-permute-start | bytes 1572872 | tf_op jit(solution)/shard_map/ppermute | solution.py:305
  74.3 5.0 %collective-permute-start.8 = (f32[2,1024]{1,0:T(2,128)S(1)}, f32[2,1024]{1,0:T(2,128)S(1)}, u32[]{:S(2)}, u32[]{:S(2)}) collective-permute-start(f32[2,1024]{1,0:T(2,128)S(1)} %get-tuple-element.86.refs_0_), channel_id=1, source_target_pairs={{0,3},{1,0},{2,1},{3,2},{4,7},{5,4},{6,5},{7,6},{8,11},{9,8},{10,9... | collective-permute-start | bytes 24584 | tf_op jit(solution)/shard_map/ppermute | solution.py:479
  77.9 4.5 %collective-permute-start.7 = (f32[2,1024]{1,0:T(2,128)S(1)}, f32[2,1024]{1,0:T(2,128)S(1)}, u32[]{:S(2)}, u32[]{:S(2)}) collective-permute-start(f32[2,1024]{1,0:T(2,128)S(1)} %get-tuple-element.86.refs_0_), channel_id=1, source_target_pairs={{0,2},{1,3},{2,0},{3,1},{4,6},{5,7},{6,4},{7,5},{8,10},{9,11},{10,... | collective-permute-start | bytes 24584 | tf_op jit(solution)/shard_map/ppermute | solution.py:479
  77.9 5.4 %collective-permute-start.6 = (f32[2,1024]{1,0:T(2,128)S(1)}, f32[2,1024]{1,0:T(2,128)S(1)}, u32[]{:S(2)}, u32[]{:S(2)}) collective-permute-start(f32[2,1024]{1,0:T(2,128)S(1)} %get-tuple-element.86.refs_0_), channel_id=1, source_target_pairs={{0,1},{1,2},{2,3},{3,0},{4,5},{5,6},{6,7},{7,4},{8,9},{9,10},{10,1... | collective-permute-start | bytes 24584 | tf_op jit(solution)/shard_map/ppermute | solution.py:479
  95.5 7.0 %collective-permute-start.9 = (f32[16,128,128]{2,1,0:T(8,128)}, f32[16,128,128]{2,1,0:T(8,128)S(1)}, u32[]{:S(2)}, u32[]{:S(2)}) collective-permute-start(f32[16,128,128]{2,1,0:T(8,128)} %get-tuple-element.88), channel_id=1, source_target_pairs={{0,4},{4,0},{8,12},{12,8},{16,20},{20,16},{24,28},{28,24},{1,5},{5... | collective-permute-start | bytes 3145736 | tf_op jit(solution)/shard_map/ppermute | solution.py:305
  95.8 6.7 %copy-start.6 = (f32[16,128,128]{2,1,0:T(8,128)S(1)}, f32[16,128,128]{2,1,0:T(8,128)}, u32[]{:S(2)}) copy-start(f32[16,128,128]{2,1,0:T(8,128)} %get-tuple-element.88) | copy-start | bytes 3145732
  102.9 20.8 %collective-permute-start.11 = (f32[4,128,128]{2,1,0:T(8,128)S(1)}, f32[4,128,128]{2,1,0:T(8,128)S(1)}, u32[]{:S(2)}, u32[]{:S(2)}) collective-permute-start(f32[4,128,128]{2,1,0:T(8,128)S(1)} %get-tuple-element.125), channel_id=1, source_target_pairs={{0,16},{4,20},{8,24},{12,28},{16,0},{20,4},{24,8},{28,12},{1,17},{... | collective-permute-start | bytes 786440 | tf_op jit(solution)/shard_map/ppermute | solution.py:305
  103.7 20.0 %collective-permute-start.10 = (f32[4,128,128]{2,1,0:T(8,128)S(1)}, f32[4,128,128]{2,1,0:T(8,128)S(1)}, u32[]{:S(2)}, u32[]{:S(2)}) collective-permute-start(f32[4,128,128]{2,1,0:T(8,128)S(1)} %get-tuple-element.126), channel_id=1, source_target_pairs={{0,8},{4,12},{8,0},{12,4},{16,24},{20,28},{24,16},{28,20},{1,9},{5... | collective-permute-start | bytes 786440 | tf_op jit(solution)/shard_map/ppermute | solution.py:305
  123.9 9.0 %collective-permute-start.12 = (f32[4,128,128]{2,1,0:T(8,128)S(1)}, f32[4,128,128]{2,1,0:T(8,128)S(1)}, u32[]{:S(2)}, u32[]{:S(2)}) collective-permute-start(f32[4,128,128]{2,1,0:T(8,128)S(1)} %get-tuple-element.124), channel_id=1, source_target_pairs={{0,16},{4,20},{8,24},{12,28},{16,0},{20,4},{24,8},{28,12},{1,17},{... | collective-permute-start | bytes 786440 | tf_op jit(solution)/shard_map/ppermute | solution.py:305
  125.4 7.9 %collective-permute-start.13 = (f32[4,128,128]{2,1,0:T(8,128)S(1)}, f32[4,128,128]{2,1,0:T(8,128)S(1)}, u32[]{:S(2)}, u32[]{:S(2)}) collective-permute-start(f32[4,128,128]{2,1,0:T(8,128)S(1)} %get-tuple-element.123), channel_id=1, source_target_pairs={{0,8},{4,12},{8,0},{12,4},{16,24},{20,28},{24,16},{28,20},{1,9},{5... | collective-permute-start | bytes 786440 | tf_op jit(solution)/shard_map/ppermute | solution.py:305
  133.6 6.8 %collective-permute-start.14 = (f32[8,128,128]{2,1,0:T(8,128)S(1)}, f32[8,128,128]{2,1,0:T(8,128)S(1)}, u32[]{:S(2)}, u32[]{:S(2)}) collective-permute-start(f32[8,128,128]{2,1,0:T(8,128)S(1)} %pad_maximum_fusion.3), channel_id=1, source_target_pairs={{0,4},{4,0},{8,12},{12,8},{16,20},{20,16},{24,28},{28,24},{1,5},{5... | collective-permute-start | bytes 1572872 | tf_op jit(solution)/shard_map/ppermute | solution.py:305

commit v3 on v2

v3 whole, which is shorter than its diff:
```python
import functools

import jax
import jax.numpy as jnp
from jax import lax
from jax.experimental import pallas as pl
from jax.experimental.pallas import tpu as pltpu
from jax.sharding import PartitionSpec as P

HEAD_TOTAL = 64
HD = 128
CHUNK = 256
GROUP = 2
WINDOWS = 4
WIDTH = HEAD_TOTAL * HD

epsilon = 1e-06
LOG2E = 1.4426950408889634

F32 = jnp.float32
BF16 = jnp.bfloat16
MIB = 1024 * 1024
NT = ((1,), (1,))


def dot(a, b, dims=((1,), (0,))):
    return lax.dot_general(a, b, (dims, ((), ())), preferred_element_type=F32)


def chunk_cumsum(x):
    lane = lax.broadcasted_iota(jnp.int32, x.shape, 1) % CHUNK
    shift = 1
    while shift < CHUNK:
        x = x + jnp.where(lane >= shift, pltpu.roll(x, shift, 1), 0.0)
        shift *= 2
    return x


def spans(chunks):
    return [slice(n * CHUNK, (n + 1) * CHUNK) for n in range(chunks)]


def state_kernel(
    chunks, heads, lc_ref, doc_ref, k_ref, v_ref,
    crow_ref, enter_ref, leave_ref, rrow_ref, cols_ref, kept_k_ref, kept_v_ref, loc_ref,
    state_ref, pass_ref,
):
    step = pl.program_id(0)

    @pl.when(step == 0)
    def _():
        c = chunk_cumsum(lc_ref[...] * LOG2E)
        r = chunk_cumsum(jnp.broadcast_to(doc_ref[...].astype(F32), (8, doc_ref.shape[1])))
        crow_ref[...] = c
        rrow_ref[...] = r
        enter = jnp.where(r[0:1] == 0.0, jnp.exp2(c), 0.0)
        enter_ref[...] = enter
        spare = jnp.zeros((HD - heads, CHUNK), F32)
        for span in spans(chunks):
            cn, rn = c[:, span], r[0:1, span]
            leave_ref[:, span] = jnp.where(rn == rn[:, -1:], jnp.exp2(cn[:, -1:] - cn), 0.0)
            cols_ref[span, :] = jnp.concatenate([cn, spare], axis=0).T

    here = pl.ds(pl.multiple_of(step * GROUP * HD, GROUP * HD), GROUP * HD)
    kept_k_ref[:, here] = k_ref[...]
    kept_v_ref[:, here] = v_ref[...]
    for g in range(GROUP):
        h = step * GROUP + g
        cols = slice(g * HD, (g + 1) * HD)
        state = None
        total = None
        for n, span in enumerate(spans(chunks)):
            keyed = (k_ref[span, cols].T.astype(F32) * leave_ref[pl.ds(h, 1), span]).astype(BF16)
            local = dot(keyed, v_ref[span, cols])
            loc_ref[h, n] = local
            passing = enter_ref[pl.ds(h, 1), span][:, CHUNK - 1 : CHUNK]
            state = local if state is None else passing * state + local
            total = passing if total is None else passing * total
        state_ref[h] = state
        pass_ref[pl.ds(h, 1), :] = jnp.broadcast_to(total, (1, HD))


def mask_kernel(rrow_ref, mask_ref):
    sub = lax.broadcasted_iota(jnp.int32, (CHUNK, CHUNK), 0)
    lane = lax.broadcasted_iota(jnp.int32, (CHUNK, CHUNK), 1)
    for n, span in enumerate(spans(mask_ref.shape[0])):
        r_row = rrow_ref[0:1, span]
        r_col = jnp.broadcast_to(r_row, (CHUNK, CHUNK)).T
        mask_ref[n] = jnp.where((r_col == r_row) & (sub <= lane), 0.0, -jnp.inf)


def weight_of(crow_ref, cols_now, mask_ref, h, g, n, span):
    c_col = jnp.broadcast_to(cols_now[span, g : g + 1], (CHUNK, CHUNK))
    return jnp.exp2(crow_ref[pl.ds(h, 1), span] - c_col + mask_ref[n])


def head_columns(cols_ref, head):
    return pltpu.roll(cols_ref[...], (HD - head) % HD, 1)


def head_span(head):
    return pl.ds(pl.multiple_of(head * HD, HD), HD)


def inside_kernel(
    chunks, first, crow_ref, cols_ref, mask_ref, k_ref, v_ref, gain_ref, q_ref, gate_ref,
    grad_ref, *refs,
):
    attn_ref, gnorm_ref, kept_q_ref, probs_ref = refs[-4:]
    step = pl.program_id(0)
    cols_now = head_columns(cols_ref, first + step * GROUP)
    for g in range(GROUP):
        h = first + step * GROUP + g
        cols = slice(g * HD, (g + 1) * HD)
        mine = head_span(h)
        for n, span in enumerate(spans(chunks)):
            q = q_ref[span, cols].T
            kept_q_ref[h, :, span] = q
            weight = weight_of(crow_ref, cols_now, mask_ref, h, g, n, span)
            probs = (dot(k_ref[span, mine], q) * weight).astype(BF16)
            probs_ref[g, n] = probs
            attn_ref[h, :, span] = dot(v_ref[span, mine].T, probs)
            sig = jax.nn.sigmoid(gate_ref[span, cols].astype(F32))
            gnorm = grad_ref[span, cols].astype(F32) * sig * gain_ref[0:1, cols]
            gnorm_ref[h, :, span] = gnorm.astype(BF16).T


def folded(x):
    return jnp.sum(x.reshape(x.shape[0] // 8, 8, x.shape[1]), axis=0)


def outside_kernel(
    chunks, enter_ref, q_ref, gnorm_ref, loc_ref, in_ref, inside_ref,
    attn_ref, held_ref, sums_ref, sq_ref, inner_ref,
):
    step = pl.program_id(0)

    @pl.when(step == 0)
    def _():
        sq_ref[...] = jnp.zeros_like(sq_ref)
        inner_ref[...] = jnp.zeros_like(inner_ref)

    heads = [step * GROUP + g for g in range(GROUP)]
    carries = [in_ref[h] for h in heads]
    for n, span in enumerate(spans(chunks)):
        squares = sq_ref[:, span]
        inners = inner_ref[:, span]
        for g, h in enumerate(heads):
            held = carries[g].astype(BF16)
            held_ref[h, n] = held
            enter = enter_ref[pl.ds(h, 1), span]
            attn = inside_ref[h, :, span] + enter * dot(held.T, q_ref[h, :, span])
            attn_ref[h, :, span] = attn
            squares = squares + folded(attn * attn)
            inners = inners + folded(gnorm_ref[h, :, span].astype(F32) * attn)
            if n + 1 < chunks:
                carries[g] = enter[:, CHUNK - 1 : CHUNK] * carries[g] + loc_ref[h, n]
        sq_ref[:, span] = squares
        inner_ref[:, span] = inners

    @pl.when(step == pl.num_programs(0) - 1)
    def _():
        sums_ref[0:1, :] = jnp.sum(sq_ref[...], axis=0, keepdims=True)
        sums_ref[1:2, :] = jnp.sum(inner_ref[...], axis=0, keepdims=True)


def grad_kernel(chunks, parts, enter_ref, *refs):
    q_ref, gnorm_ref, attn_ref, _, agrad_ref, bloc_ref, back_ref, scale_ref = refs[parts:]
    step = pl.program_id(0)

    @pl.when(step == 0)
    def _():
        sums = refs[0][...]
        for ref in refs[1:parts]:
            sums = sums + ref[...]
        inverse = lax.rsqrt(sums[0:1] / WIDTH + epsilon)
        scale_ref[0:1, :] = inverse
        scale_ref[1:2, :] = inverse * inverse * inverse * sums[1:2] / WIDTH

    for g in range(GROUP):
        h = step * GROUP + g
        back = None
        for n, span in reversed(list(enumerate(spans(chunks)))):
            enter = enter_ref[pl.ds(h, 1), span]
            gnorm = gnorm_ref[h, :, span].astype(F32)
            agrad = scale_ref[0:1, span] * gnorm - attn_ref[h, :, span] * scale_ref[1:2, span]
            agrad = agrad.astype(BF16)
            agrad_ref[h, :, span] = agrad
            qkeyed = (q_ref[h, :, span].astype(F32) * enter).astype(BF16)
            local = dot(qkeyed, agrad, NT)
            bloc_ref[h, n] = local
            back = local if back is None else local + enter[:, CHUNK - 1 : CHUNK] * back
        back_ref[h] = back


def inner_grad_kernel(
    chunks, first, crow_ref, enter_ref, scale_ref, cols_ref, mask_ref, k_ref, v_ref, attn_ref,
    held_ref, q_ref, agrad_ref, gain_ref, gate_ref, grad_ref, probs_ref, *refs,
):
    dk_ref, dv_ref, dq_ref, gated_ref, ggate_ref = refs[-5:]
    step = pl.program_id(0)
    cols_now = head_columns(cols_ref, first + step * GROUP)
    for g in range(GROUP):
        h = first + step * GROUP + g
        cols = slice(g * HD, (g + 1) * HD)
        mine = head_span(h)
        for n, span in enumerate(spans(chunks)):
            q, agrad = q_ref[h, :, span], agrad_ref[h, :, span]
            k, v = k_ref[span, mine], v_ref[span, mine]
            weight = weight_of(crow_ref, cols_now, mask_ref, h, g, n, span)
            both = dot(jnp.concatenate([v, held_ref[h, n]], axis=0), agrad)
            dscore = (both[:CHUNK] * weight).astype(BF16)
            dq = dot(k.T, dscore) + enter_ref[pl.ds(h, 1), span] * both[CHUNK:]
            dq_ref[span, cols] = dq.astype(BF16).T
            dv_ref[h, :, span] = dot(agrad, probs_ref[g, n], NT).astype(BF16)
            dk_ref[h, :, span] = dot(q, dscore, NT).astype(BF16)
            normed = (attn_ref[h, :, span] * scale_ref[0:1, span]).T * gain_ref[0:1, cols]
            sig = jax.nn.sigmoid(gate_ref[span, cols].astype(F32))
            gated = normed * sig
            gated_ref[span, cols] = gated.astype(BF16)
            ggate = grad_ref[span, cols].astype(F32) * gated * (1.0 - sig)
            ggate_ref[span, cols] = ggate.astype(BF16)


def outer_grad_kernel(
    chunks, enter_ref, leave_ref, k_ref, v_ref, dkin_ref, dvin_ref, bloc_ref, out_ref,
    dk_ref, dv_ref,
):
    step = pl.program_id(0)
    for g in range(GROUP):
        h = step * GROUP + g
        cols = slice(g * HD, (g + 1) * HD)
        mine = head_span(h)
        carry = out_ref[h]
        for n, span in reversed(list(enumerate(spans(chunks)))):
            leave = leave_ref[pl.ds(h, 1), span]
            back = carry.astype(BF16)
            dk = dkin_ref[h, :, span].astype(F32) + leave * dot(back, v_ref[span, mine], NT)
            dv = dvin_ref[h, :, span].astype(F32) + leave * dot(back.T, k_ref[span, mine], NT)
            dk_ref[span, cols] = dk.astype(BF16).T
            dv_ref[span, cols] = dv.astype(BF16).T
            if n > 0:
                passing = enter_ref[pl.ds(h, 1), span][:, CHUNK - 1 : CHUNK]
                carry = bloc_ref[h, n] + passing * carry


def hbm(x):
    return pltpu.with_memory_space_constraint(x, pltpu.HBM)


def kept(*arrays):
    spec = pl.BlockSpec(memory_space=pltpu.VMEM)
    return [(pltpu.with_memory_space_constraint(x, pltpu.VMEM), spec) for x in arrays]


def keep(dims, dtype):
    return pltpu.VMEM(dims, dtype), pl.BlockSpec(memory_space=pltpu.VMEM)


def call(kernel, grid, ins, outs, scratch=(), aliases=None, room=8, flops=0, moved=0, exps=0):
    return pl.pallas_call(
        kernel,
        grid=grid,
        in_specs=[spec for _, spec in ins],
        out_specs=[spec for _, spec in outs],
        out_shape=[shape for shape, _ in outs],
        scratch_shapes=list(scratch),
        input_output_aliases=aliases or {},
        compiler_params=pltpu.CompilerParams(
            dimension_semantics=("arbitrary",) * len(grid), vmem_limit_bytes=room * MIB
        ),
        cost_estimate=pl.CostEstimate(flops=flops, bytes_accessed=moved, transcendentals=exps),
    )(*[x for x, _ in ins])


def after(x, *others):
    return lax.optimization_barrier((x, *others))[0]


def across(x, flips, devices=8):
    return lax.ppermute(x, "seq", [(i, i ^ flips) for i in range(devices)])


def cube_scan(state, own_pass, passes, index, fill):
    heads = state.shape[0]
    half, quarter = heads // 2, heads // 4
    core, x, y = index % 2, (index // 2) % 2, index // 4
    factor = lambda rows: rows[:, None, :]
    mine = lambda a: lax.dynamic_slice_in_dim(a, core * half, half, 0)

    other = across(state, 1)
    beside_pass = passes[0] if passes else across(own_pass, 1)
    other, beside_pass = lax.optimization_barrier((other, beside_pass, fill(0, state)))[:2]
    early = jnp.where(core == 0, state, other)
    late = jnp.where(core == 0, other, state)
    early_pass = jnp.where(core == 0, own_pass, beside_pass)
    late_pass = jnp.where(core == 0, beside_pass, own_pass)
    total = factor(mine(late_pass)) * mine(early) + mine(late)
    to_x, to_y = total[:quarter], total[quarter:]

    chip_pass = own_pass * beside_pass
    from_x, from_y = across(to_x, 2), across(to_y, 4)
    x_pass, far_pass = passes[1:] if passes else (across(chip_pass, 2), across(chip_pass, 6))
    from_x, from_y, x_pass, far_pass = lax.optimization_barrier(
        (from_x, from_y, x_pass, far_pass, fill(1, total))
    )[:4]
    chip_x, chip_y = mine(chip_pass)[:quarter], mine(chip_pass)[quarter:]
    side_x, side_y = mine(x_pass)[:quarter], mine(x_pass)[quarter:]
    far_y = mine(far_pass)[quarter:]
    left = jnp.where(x == 0, to_x, from_x)
    right = jnp.where(x == 0, from_x, to_x)
    row = factor(jnp.where(x == 0, side_x, chip_x)) * left + right
    through = factor(chip_y) * (factor(far_y) * from_y) + to_y
    sent = jnp.where(y == 0, to_y, jnp.where(x == 0, through, from_y))

    row_in, sent_in = across(row, 4), across(sent, 2)
    row_in, sent_in = lax.optimization_barrier((row_in, sent_in, fill(2, sent)))[:2]
    lower = jnp.where(x == 0, row_in, factor(side_x) * row_in + from_x)
    upper = jnp.where(x == 0, 0.0, from_x)
    in_x = jnp.where(y == 0, upper, lower)
    more = factor(jnp.where(x == 0, far_y, side_y)) * from_y
    in_y = jnp.where(y == 0, jnp.where(x == 0, 0.0, sent_in), more + sent_in)
    ahead = jnp.concatenate([in_x, in_y], axis=0)

    beside = across(ahead, 1)
    beside = after(beside, fill(3, ahead))
    low = jnp.where(core == 0, ahead, beside)
    high = jnp.where(core == 0, beside, ahead)
    entering = jnp.concatenate([low, high], axis=0)
    entering = jnp.where(core == 0, entering, factor(early_pass) * entering + early)
    return entering, (beside_pass, x_pass, far_pass)


def doubling_scan(state, own_pass, fill, reverse):
    devices = lax.axis_size("seq")
    index = lax.axis_index("seq")
    passes = lax.all_gather(own_pass, "seq")
    if reverse:
        passes = passes[::-1]
        index = devices - 1 - index
    route = lambda hop: [
        (i, i - hop if reverse else i + hop)
        for i in range(devices)
        if 0 <= (i - hop if reverse else i + hop) < devices
    ]
    for window in range(WINDOWS):
        state = after(state, fill(window, state))
    hop = 1
    while hop < devices:
        factor = lax.dynamic_index_in_dim(passes, index, 0, False)
        state = factor[:, None, :] * lax.ppermute(state, "seq", route(hop)) + state
        before = jnp.concatenate([jnp.zeros_like(passes[:hop]), passes[:-hop]], axis=0)
        passes = passes * before
        hop *= 2
    return lax.ppermute(state, "seq", route(1))


def scan_devices(state, own_pass, passes, fill, reverse):
    devices = lax.axis_size("seq")
    if devices == 8 and state.shape[0] % 4 == 0:
        index = lax.axis_index("seq")
        index = devices - 1 - index if reverse else index
        return cube_scan(state, own_pass, passes, index, fill)
    return doubling_scan(state, own_pass, fill, reverse), None


def body(queries, key_rows, value_rows, log_decay, doc_start, gate_input, norm_gain, out_grad):
    rows, cols = queries.shape
    heads = cols // HD
    chunks = rows // CHUNK
    parts = lax.axis_size("head")
    grid = (heads // GROUP,)
    share = heads // WINDOWS
    big = rows * cols * 2
    tile = 2 * rows * CHUNK * cols
    small = 2 * rows * HD * cols

    whole = lambda *dims: pl.BlockSpec(dims, lambda i: (0,) * len(dims))
    anywhere = pl.BlockSpec(memory_space=pl.ANY)

    def wide(base=0):
        return pl.BlockSpec((rows, GROUP * HD), lambda i: (0, i + base // GROUP))

    def gain_spec(base=0):
        return pl.BlockSpec((1, GROUP * HD), lambda i: (0, i + base // GROUP))

    probs_spec = pl.BlockSpec((GROUP, chunks, CHUNK, CHUNK), lambda i: (i, 0, 0, 0))
    by_head = (heads, HD, rows)
    local_dims = (heads, chunks, HD, HD)
    wide_shape = pltpu.HBM((rows, cols), BF16)
    queries, key_rows, value_rows, gate_input, out_grad = map(
        hbm, (queries, key_rows, value_rows, gate_input, out_grad)
    )
    doc_row = doc_start.reshape(1, rows)
    gain_row = norm_gain.reshape(1, cols)

    crow, enter, leave, rrow, columns, keys, values, local, state, own_pass = call(
        functools.partial(state_kernel, chunks, heads),
        grid,
        [
            (log_decay, whole(heads, rows)), (doc_row, whole(1, rows)),
            (key_rows, wide()), (value_rows, wide()),
        ],
        [keep((heads, rows), F32)] * 3
        + [
            keep((8, rows), F32), keep((rows, HD), F32), keep((rows, cols), BF16),
            keep((rows, cols), BF16), keep(local_dims, F32), keep((heads, HD, HD), F32),
            keep((heads, HD), F32),
        ],
        flops=small, moved=2 * big,
    )

    mask = []
    made = []
    probs = []

    def fill_forward(window, tie):
        base = window * share
        if not mask:
            mask[:] = call(
                mask_kernel, (), kept(after(rrow, tie)), [keep((chunks, CHUNK, CHUNK), F32)],
                flops=8 * rows * CHUNK,
            )
        ins = kept(after(crow, tie), columns, mask[0], keys, values) + [
            (gain_row, gain_spec(base)), (queries, wide(base)), (gate_input, wide(base)),
            (out_grad, wide(base)),
        ]
        aliases = {len(ins) + i: i for i in range(len(made))}
        ins += kept(*made)
        *made[:], fresh = call(
            functools.partial(inside_kernel, chunks, base),
            (share // GROUP,),
            ins,
            [
                keep(by_head, F32), keep(by_head, BF16), keep(by_head, BF16),
                (pltpu.HBM((share, chunks, CHUNK, CHUNK), BF16), probs_spec),
            ],
            aliases=aliases, room=12,
            flops=2 * tile // WINDOWS, moved=5 * big // WINDOWS,
            exps=rows * (CHUNK + HD) * heads // WINDOWS,
        )
        probs.append(fresh)
        return fresh

    incoming, passes = scan_devices(state, own_pass, None, fill_forward, False)
    inside, gnorm, turned = made

    attn, held, sums = call(
        functools.partial(outside_kernel, chunks),
        grid,
        kept(enter, turned, gnorm, local, incoming, inside),
        [keep(by_head, F32), keep(local_dims, BF16), keep((2, rows), F32)],
        [pltpu.VMEM((8, rows), F32)] * 2,
        {5: 0},
        flops=small, moved=big,
    )

    all_sums = [sums]
    for hop in range(1, parts):
        route = [(i, (i + hop) % parts) for i in range(parts)]
        all_sums.append(lax.ppermute(sums, "head", route))

    agrad, bloc, back, scales = call(
        functools.partial(grad_kernel, chunks, parts),
        grid,
        kept(enter, *all_sums, turned, gnorm, attn, local),
        [
            keep(by_head, BF16), keep(local_dims, F32), keep((heads, HD, HD), F32),
            keep((2, rows), F32),
        ],
        aliases={parts + 4: 1},
        flops=small, moved=big,
    )

    inner = [turned, agrad]
    outs = []

    def fill_backward(window, tie):
        base = window * share
        ins = kept(
            after(crow, tie), enter, scales, columns, mask[0], keys, values, attn, held, *inner
        )
        aliases = {len(ins) - 2: 0, len(ins) - 1: 1}
        ins += [
            (gain_row, gain_spec(base)), (gate_input, wide(base)), (out_grad, wide(base)),
            (hbm(probs[window]), probs_spec),
        ]
        aliases.update({len(ins) + i: 2 + i for i in range(len(outs))})
        ins += [(hbm(x), anywhere) for x in outs]
        inner[0], inner[1], *outs[:] = call(
            functools.partial(inner_grad_kernel, chunks, base),
            (share // GROUP,),
            ins,
            [keep(by_head, BF16)] * 2 + [(wide_shape, wide(base))] * 3,
            aliases=aliases, room=14,
            flops=(4 * tile + small) // WINDOWS, moved=7 * big // WINDOWS,
            exps=rows * (CHUNK + HD) * heads // WINDOWS,
        )
        return outs[0]

    outgoing, _ = scan_devices(back, own_pass, passes, fill_backward, True)
    dq, gated, gate_grad = outs

    dk, dv = call(
        functools.partial(outer_grad_kernel, chunks),
        grid,
        kept(enter, leave, keys, values, *inner, bloc, outgoing),
        [(wide_shape, wide())] * 2,
        flops=2 * small, moved=2 * big,
    )
    return (gated, gate_grad, dq, dk, dv)


def solution(mesh):
    in_specs = (
        P("seq", "head"),
        P("seq", "head"),
        P("seq", "head"),
        P("head", "seq"),
        P("seq"),
        P("seq", "head"),
        P("head"),
        P("seq", "head"),
    )
    out_specs = (P("seq", "head"),) * 5
    return jax.shard_map(body, mesh=mesh, in_specs=in_specs, out_specs=out_specs, check_vma=False)
```

time: 157 us -> 196 us (1.25)
  local copies, waits for them, and re-layouts: 2.71 us -> 72.8 us
  Pallas kernels: 112 us -> 91.6 us
  blocking collectives: 15.3 us -> 0 us
  starting transfers between devices: 12.8 us -> 18.1 us
    unnamed x18 -> x92, local copies, waits for them, and re-layouts: 2.13 us -> 72.7 us
    pallas_call x13, Pallas kernels: 112 us -> 91.6 us  [call(): pl.pallas_call(kernel, grid=grid, in_specs=[spec for _, spec in ins], out...]
    unnamed x1 -> x0, blocking collectives: 15.3 us -> none
    ppermute x15 -> x18, starting transfers between devices: 12.8 us -> 18.1 us  [the longest x15 13.5 us: across(): return lax.ppermute(x, 'seq', [(i, i ^ flips) for i in range(devices)])]
    add x2, other arithmetic: 0.26 us -> 2.99 us  [cube_scan(): total = factor(mine(late_pass)) * mine(early) + mine(late)]
    select_n x4 -> x5, other arithmetic: 2.51 us -> 0.34 us  [the longest x2 0.32 us: cube_scan(): jnp.where(core == 0, entering, factor(early_pass) * entering + early)]
    ppermute x15 -> x18, waiting for transfers between devices: 5.74 us -> 5.56 us  [the longest x3 4.44 us: body(): all_sums.append(lax.ppermute(sums, 'head', route))]
  transfers between devices with their start and end apart: 15 -> 18, of which waited for: 6 -> 4; matrix products, arithmetic and copies ran while one was open for 2% -> 0% of each run, Pallas kernels for 39% -> 35%
where the time goes in v3:
time: 196 us; the launch traced here: 195 us
  Pallas kernels  91.6 us (47%)
  local copies, waits for them, and re-layouts  72.8 us (37%)
  starting transfers between devices  18.1 us (9%)
  waiting for transfers between devices  5.56 us (3%)
  other arithmetic  5.45 us (3%)
    pallas_call x13, Pallas kernels, call(): pl.pallas_call(kernel, grid=grid, in_specs=[spec for _, spec in ins], out...  91.6 us
    unnamed x92, local copies, waits for them, and re-layouts  72.7 us
    ppermute x15, starting transfers between devices, across(): return lax.ppermute(x, 'seq', [(i, i ^ flips) for i in range(devices)])  13.5 us
    ppermute x3, starting transfers between devices, body(): all_sums.append(lax.ppermute(sums, 'head', route))  4.67 us
    ppermute x3, waiting for transfers between devices, body(): all_sums.append(lax.ppermute(sums, 'head', route))  4.44 us
  transfers between devices with their start and end apart: 18, of which 4 were waited for; matrix products, arithmetic and copies ran while one was open for 0% of the time, Pallas kernels for 35%

profile of v3, /device:TPU:0, one launch (start us, length us, event | category | flops | bytes accessed | tf_op | source)
XLA Modules:
  0.0 194.6 jit_solution(3212473661107963421)
XLA Ops:
  2.2 8.8 %shard_map.119 = (f32[16,1024]{1,0:T(8,128)S(1)}, f32[16,1024]{1,0:T(8,128)S(1)}, f32[16,1024]{1,0:T(8,128)S(1)}, f32[8,1024]{1,0:T(8,128)S(1)}, f32[1024,128]{1...) custom-call(f32[16,1024]{1,0:T(8,128)S(1)} %copy-done.40, ...), custom_call_target="tpu_custom_call" | custom-call | flops 536870912 | bytes 8388608 | tf_op jit(solution)/shard_map/pallas_call | solution.py:261
  13.7 7.5 %shard_map.121 = (f32[16,128,1024]{2,1,0:T(8,128)S(1)}, bf16[16,128,1024]{2,1,0:T(8,128)(2,1)S(1)}, bf16[16,128,1024]{2,1,0:T(8,128)(2,1)S(1)}, bf16[4,4,256,256]{3,2,1,0:T(8,128)(2,1)}) custom-call(f32[16,1024]{1,0:T(8,128)S(1)} %get-tuple-element.154.crow_ref, f32[1024,128]{1,0:T(8,128)S(1)} %get-tuple-element.92.cols_ref, ...), custom_call_target="tpu_custom_call" | custom-call | flops 536870912 | bytes 5242880 | tf_op jit(solution)/shard_map/pallas_call | solution.py:261
  21.2 3.4 %copy-done = f32[16,128,1024]{2,1,0:T(8,128)} copy-done((f32[16,128,1024]{2,1,0:T(8,128)}, f32[16,128,1024]{2,1,0:T(8,128)S(1)}, u32[]{:S(2)}) %copy-start) | copy-done | bytes 8388632
  30.3 3.0 %collective-permute-start.3 = (f32[4,128,128]{2,1,0:T(8,128)S(1)}, f32[4,128,128]{2,1,0:T(8,128)S(1)}, u32[]{:S(2)}, u32[]{:S(2)}) collective-permute-start(f32[4,128,128]{2,1,0:T(8,128)S(1)} %get-tuple-element.179), channel_id=1, source_target_pairs={{0,16},{4,20},{8,24},{12,28},{16,0},{20,4},{24,8},{28,12},{1,17},{... | collective-permute-start | bytes 786440 | tf_op jit(solution)/shard_map/ppermute | solution.py:281
  36.8 3.4 %copy-done.1 = f32[16,128,1024]{2,1,0:T(8,128)S(1)} copy-done((f32[16,128,1024]{2,1,0:T(8,128)S(1)}, f32[16,128,1024]{2,1,0:T(8,128)}, u32[]{:S(2)}) %copy-start.1) | copy-done | bytes 8388632
  40.2 2.2 %copy-done.8 = bf16[16,128,1024]{2,1,0:T(8,128)(2,1)S(1)} copy-done((bf16[16,128,1024]{2,1,0:T(8,128)(2,1)S(1)}, bf16[16,128,1024]{2,1,0:T(8,128)(2,1)}, u32[]{:S(2)}) %copy-start.8) | copy-done | bytes 4194328
  42.4 2.2 %copy-done.14 = bf16[1024,2048]{1,0:T(8,128)(2,1)S(1)} copy-done((bf16[1024,2048]{1,0:T(8,128)(2,1)S(1)}, bf16[1024,2048]{1,0:T(8,128)(2,1)}, u32[]{:S(2)}) %copy-start.14) | copy-done | bytes 4194328
  49.0 6.4 %shard_map.122 = (f32[16,128,1024]{2,1,0:T(8,128)S(1)}, bf16[16,128,1024]{2,1,0:T(8,128)(2,1)S(1)}, bf16[16,128,1024]{2,1,0:T(8,128)(2,1)S(1)}, bf16[4,4,256,256]{3,2,1,0:T(8,128)(2,1)}) custom-call(f32[16,1024]{1,0:T(8,128)S(1)} %get-tuple-element.154.crow_ref, ...), custom_call_target="tpu_custom_call", output_to_operand_aliasing={{0}: (9, {}), {1}: (10, {}), {2}: (11, {})} | custom-call | flops 536870912 | bytes 5242880 | tf_op jit(solution)/shard_map/pallas_call | solution.py:261
  57.7 6.4 %shard_map.123 = (f32[16,128,1024]{2,1,0:T(8,128)S(1)}, bf16[16,128,1024]{2,1,0:T(8,128)(2,1)S(1)}, bf16[16,128,1024]{2,1,0:T(8,128)(2,1)S(1)}, bf16[4,4,256,256]{3,2,1,0:T(8,128)(2,1)}) custom-call(f32[16,1024]{1,0:T(8,128)S(1)} %get-tuple-element.154.crow_ref, ...), custom_call_target="tpu_custom_call", output_to_operand_aliasing={{0}: (9, {}), {1}: (10, {}), {2}: (11, {})} | custom-call | flops 536870912 | bytes 5242880 | tf_op jit(solution)/shard_map/pallas_call | solution.py:261
  65.4 6.5 %shard_map.124 = (f32[16,128,1024]{2,1,0:T(8,128)S(1)}, bf16[16,128,1024]{2,1,0:T(8,128)(2,1)S(1)}, bf16[16,128,1024]{2,1,0:T(8,128)(2,1)S(1)}, bf16[4,4,256,256]{3,2,1,0:T(8,128)(2,1)}) custom-call(f32[16,1024]{1,0:T(8,128)S(1)} %get-tuple-element.154.crow_ref, ...), custom_call_target="tpu_custom_call", output_to_operand_aliasing={{0}: (9, {}), {1}: (10, {}), {2}: (11, {})} | custom-call | flops 536870912 | bytes 5242880 | tf_op jit(solution)/shard_map/pallas_call | solution.py:261
  71.9 3.4 %copy-done.2 = f32[16,128,1024]{2,1,0:T(8,128)} copy-done((f32[16,128,1024]{2,1,0:T(8,128)}, f32[16,128,1024]{2,1,0:T(8,128)S(1)}, u32[]{:S(2)}) %copy-start.2) | copy-done | bytes 8388632
  77.5 3.4 %copy-done.31 = bf16[16,128,1024]{2,1,0:T(8,128)(2,1)S(1)} copy-done((bf16[16,128,1024]{2,1,0:T(8,128)(2,1)S(1)}, bf16[16,128,1024]{2,1,0:T(8,128)(2,1)}, u32[]{:S(2)}) %copy-start.31) | copy-done | bytes 4194328
  81.0 3.4 %copy-done.3 = f32[16,128,1024]{2,1,0:T(8,128)S(1)} copy-done((f32[16,128,1024]{2,1,0:T(8,128)S(1)}, f32[16,128,1024]{2,1,0:T(8,128)}, u32[]{:S(2)}) %copy-start.3) | copy-done | bytes 8388632
  84.3 4.4 %shard_map.125 = (f32[16,128,1024]{2,1,0:T(8,128)S(1)}, bf16[16,4,128,128]{3,2,1,0:T(8,128)(2,1)S(1)}, f32[2,1024]{1,0:T(2,128)S(1)}) custom-call(f32[16,1024]{1,0:T(8,128)S(1)} %get-tuple-element.88.enter_ref, bf16[16,128,1024]{2,1,0:T(8,128)(2,1)S(1)} %get-tuple-element.120.q_ref.refs_4_, ...), custom_call_target="tpu_custom_call", output_to_operand_aliasing={{0}: (5, {})} | custom-call | flops 536870912 | bytes 4194304 | tf_op jit(solution)/shard_map/pallas_call | solution.py:261
  88.7 3.7 %collective-permute-start.11 = (f32[2,1024]{1,0:T(2,128)S(1)}, f32[2,1024]{1,0:T(2,128)S(1)}, u32[]{:S(2)}, u32[]{:S(2)}) collective-permute-start(f32[2,1024]{1,0:T(2,128)S(1)} %get-tuple-element.126.refs_0_), channel_id=1, source_target_pairs={{0,3},{1,0},{2,1},{3,2},{4,7},{5,4},{6,5},{7,6},{8,11},{9,8},{10,9... | collective-permute-start | bytes 24584 | tf_op jit(solution)/shard_map/ppermute | solution.py:461
  93.8 3.2 %collective-permute-done.10.refs_2_ = f32[2,1024]{1,0:T(2,128)S(1)} collective-permute-done((f32[2,1024]{1,0:T(2,128)S(1)}, f32[2,1024]{1,0:T(2,128)S(1)}, u32[]{:S(2)}, u32[]{:S(2)}) %collective-permute-start.10) | collective-permute-done | bytes 8224 | tf_op jit(solution)/shard_map/ppermute | solution.py:461
  97.8 3.4 %shard_map.126 = (bf16[16,128,1024]{2,1,0:T(8,128)(2,1)S(1)}, f32[16,4,128,128]{3,2,1,0:T(8,128)S(1)}, f32[16,128,128]{2,1,0:T(8,128)S(1)}, f32[2,1024]{1,0:T(2,128)S(1)}) custom-call(f32[16,1024]{1,0:T(8,128)S(1)} %get-tuple-element.88.enter_ref, f32[2,1024]{1,0:T(2,128)S(1)} %get-tuple-element.126.refs_0_, ...), custom_call_target="tpu_custom_call", output_to_operand_aliasing={{1}: (8, {})} | custom-call | flops 536870912 | bytes 4194304 | tf_op jit(solution)/shard_map/pallas_call | solution.py:261
  105.4 3.4 %copy-done.5 = f32[16,128,1024]{2,1,0:T(8,128)S(1)} copy-done((f32[16,128,1024]{2,1,0:T(8,128)S(1)}, f32[16,128,1024]{2,1,0:T(8,128)}, u32[]{:S(2)}) %copy-start.5) | copy-done | bytes 8388632
  119.1 10.0 %shard_map.127 = (bf16[16,128,1024]{2,1,0:T(8,128)(2,1)S(1)}, bf16[16,128,1024]{2,1,0:T(8,128)(2,1)S(1)}, bf16[1024,2048]{1,0:T(8,128)(2,1)}, bf16[1024,2048]{1,0:T(8,128)(2,1)}, bf16[1024,2048]{1,0:T(8,128)(2,1)}) custom-call(f32[16,1024]{1,0:T(8,128)S(1)} %get-tuple-element.154.crow_ref, ...), custom_call_target="tpu_custom_call", output_to_operand_aliasing={{0}: (9, {}), {1}: (10, {})} | custom-call | flops 1207959552 | bytes 7340032 | tf_op jit(solution)/shard_map/pallas_call | solution.py:261
  137.1 3.4 %copy-done.6 = f32[16,128,1024]{2,1,0:T(8,128)S(1)} copy-done((f32[16,128,1024]{2,1,0:T(8,128)S(1)}, f32[16,128,1024]{2,1,0:T(8,128)}, u32[]{:S(2)}) %copy-start.6) | copy-done | bytes 8388632
  150.8 10.0 %shard_map.128 = (bf16[16,128,1024]{2,1,0:T(8,128)(2,1)S(1)}, bf16[16,128,1024]{2,1,0:T(8,128)(2,1)S(1)}, bf16[1024,2048]{1,0:T(8,128)(2,1)}, bf16[1024,2048]{1,0:T(8,128)(2,1)}, bf16[1024,2048]{1,0:T(8,128)(2,1)}) custom-call(f32[16,1024]{1,0:T(8,128)S(1)} %get-tuple-element.154.crow_, ...), custom_call_target="tpu_custom_call", output_to_operand_aliasing={{0}: (9, {}), {1}: (10, {}), {2}: (15, {}), {3}: (16, {}), ... | custom-call | flops 1207959552 | bytes 7340032 | tf_op jit(solution)/shard_map/pallas_call | solution.py:261
  164.0 10.0 %shard_map.129 = (bf16[16,128,1024]{2,1,0:T(8,128)(2,1)S(1)}, bf16[16,128,1024]{2,1,0:T(8,128)(2,1)S(1)}, bf16[1024,2048]{1,0:T(8,128)(2,1)}, bf16[1024,2048]{1,0:T(8,128)(2,1)}, bf16[1024,2048]{1,0:T(8,128)(2,1)}) custom-call(f32[16,1024]{1,0:T(8,128)S(1)} %get-tuple-element.154.crow_, ...), custom_call_target="tpu_custom_call", output_to_operand_aliasing={{0}: (9, {}), {1}: (10, {}), {2}: (15, {}), {3}: (16, {}), ... | custom-call | flops 1207959552 | bytes 7340032 | tf_op jit(solution)/shard_map/pallas_call | solution.py:261
  174.3 10.4 %shard_map.130 = (bf16[16,128,1024]{2,1,0:T(8,128)(2,1)S(1)}, bf16[16,128,1024]{2,1,0:T(8,128)(2,1)S(1)}, bf16[1024,2048]{1,0:T(8,128)(2,1)}, bf16[1024,2048]{1,0:T(8,128)(2,1)}, bf16[1024,2048]{1,0:T(8,128)(2,1)}) custom-call(f32[16,1024]{1,0:T(8,128)S(1)} %get-tuple-element.154.crow_, ...), custom_call_target="tpu_custom_call", output_to_operand_aliasing={{0}: (9, {}), {1}: (10, {}), {2}: (15, {}), {3}: (16, {}), ... | custom-call | flops 1207959552 | bytes 7340032 | tf_op jit(solution)/shard_map/pallas_call | solution.py:261
  186.9 7.7 %shard_map.131 = (bf16[1024,2048]{1,0:T(8,128)(2,1)}, bf16[1024,2048]{1,0:T(8,128)(2,1)}) custom-call(f32[16,1024]{1,0:T(8,128)S(1)} %get-tuple-element.88.enter_ref, f32[16,1024]{1,0:T(8,128)S(1)} %get-tuple-element.162.leave_ref, bf16[1024,2048]{1,0:T(8,128)(2,1)S(1)} %copy-done.18, bf16[1024,2048]{1,0:T(8,128)(2,1)S(1)} %copy-done.23, ...), custom_call_target="tpu_custom_call" | custom-call | flops 1073741824 | bytes 8388608 | tf_op jit(solution)/shard_map/pallas_call | solution.py:261
  (145 shorter events, 64.2 us)
Async XLA Ops:
  2.2 11.5 %copy-start.39 = (f32[2048]{0:T(1024)S(1)}, f32[2048]{0:T(1024)}, u32[]{:S(2)}) copy-start(f32[2048]{0:T(1024)} %param.14) | copy-start | bytes 24580
  13.0 15.7 %collective-permute-start = (f32[16,128,128]{2,1,0:T(8,128)S(1)}, f32[16,128,128]{2,1,0:T(8,128)}, u32[]{:S(2)}, u32[]{:S(2)}) collective-permute-start(f32[16,128,128]{2,1,0:T(8,128)S(1)} %get-tuple-element.89), channel_id=1, source_target_pairs={{0,4},{4,0},{8,12},{12,8},{16,20},{20,16},{24,28},{28,24},{1,5},{5... | collective-permute-start | bytes 3145736 | tf_op jit(solution)/shard_map/ppermute | solution.py:281
  13.4 15.2 %collective-permute-start.1 = (f32[16,128]{1,0:T(8,128)S(1)}, f32[16,128]{1,0:T(8,128)S(1)}, u32[]{:S(2)}, u32[]{:S(2)}) collective-permute-start(f32[16,128]{1,0:T(8,128)S(1)} %get-tuple-element.90), channel_id=1, source_target_pairs={{0,4},{4,0},{8,12},{12,8},{16,20},{20,16},{24,28},{28,24},{1,5},{5... | collective-permute-start | bytes 24584 | tf_op jit(solution)/shard_map/ppermute | solution.py:281
  30.3 25.1 %collective-permute-start.3 = (f32[4,128,128]{2,1,0:T(8,128)S(1)}, f32[4,128,128]{2,1,0:T(8,128)S(1)}, u32[]{:S(2)}, u32[]{:S(2)}) collective-permute-start(f32[4,128,128]{2,1,0:T(8,128)S(1)} %get-tuple-element.179), channel_id=1, source_target_pairs={{0,16},{4,20},{8,24},{12,28},{16,0},{20,4},{24,8},{28,12},{1,17},{... | collective-permute-start | bytes 786440 | tf_op jit(solution)/shard_map/ppermute | solution.py:281
  33.4 22.1 %collective-permute-start.2 = (f32[4,128,128]{2,1,0:T(8,128)S(1)}, f32[4,128,128]{2,1,0:T(8,128)S(1)}, u32[]{:S(2)}, u32[]{:S(2)}) collective-permute-start(f32[4,128,128]{2,1,0:T(8,128)S(1)} %get-tuple-element.180), channel_id=1, source_target_pairs={{0,8},{4,12},{8,0},{12,4},{16,24},{20,28},{24,16},{28,20},{1,9},{5... | collective-permute-start | bytes 786440 | tf_op jit(solution)/shard_map/ppermute | solution.py:281
  34.8 20.6 %collective-permute-start.5 = (f32[16,128]{1,0:T(8,128)S(1)}, f32[16,128]{1,0:T(8,128)S(1)}, u32[]{:S(2)}, u32[]{:S(2)}) collective-permute-start(f32[16,128]{1,0:T(8,128)S(1)} %get-tuple-element.184), channel_id=1, source_target_pairs={{0,24},{4,28},{8,16},{12,20},{16,8},{20,12},{24,0},{28,4},{1,25},{... | collective-permute-start | bytes 24584 | tf_op jit(solution)/shard_map/ppermute | solution.py:281
  34.9 20.5 %collective-permute-start.4 = (f32[16,128]{1,0:T(8,128)S(1)}, f32[16,128]{1,0:T(8,128)S(1)}, u32[]{:S(2)}, u32[]{:S(2)}) collective-permute-start(f32[16,128]{1,0:T(8,128)S(1)} %get-tuple-element.184), channel_id=1, source_target_pairs={{0,8},{4,12},{8,0},{12,4},{16,24},{20,28},{24,16},{28,20},{1,9},{5... | collective-permute-start | bytes 24584 | tf_op jit(solution)/shard_map/ppermute | solution.py:281
  55.6 8.5 %collective-permute-start.6 = (f32[4,128,128]{2,1,0:T(8,128)S(1)}, f32[4,128,128]{2,1,0:T(8,128)S(1)}, u32[]{:S(2)}, u32[]{:S(2)}) collective-permute-start(f32[4,128,128]{2,1,0:T(8,128)S(1)} %get-tuple-element.178), channel_id=1, source_target_pairs={{0,16},{4,20},{8,24},{12,28},{16,0},{20,4},{24,8},{28,12},{1,17},{... | collective-permute-start | bytes 786440 | tf_op jit(solution)/shard_map/ppermute | solution.py:281
  57.2 8.0 %collective-permute-start.7 = (f32[4,128,128]{2,1,0:T(8,128)S(1)}, f32[4,128,128]{2,1,0:T(8,128)S(1)}, u32[]{:S(2)}, u32[]{:S(2)}) collective-permute-start(f32[4,128,128]{2,1,0:T(8,128)S(1)} %get-tuple-element.177), channel_id=1, source_target_pairs={{0,8},{4,12},{8,0},{12,4},{16,24},{20,28},{24,16},{28,20},{1,9},{5... | collective-permute-start | bytes 786440 | tf_op jit(solution)/shard_map/ppermute | solution.py:281
  65.3 11.9 %collective-permute-start.8 = (f32[8,128,128]{2,1,0:T(8,128)S(1)}, f32[8,128,128]{2,1,0:T(8,128)S(1)}, u32[]{:S(2)}, u32[]{:S(2)}) collective-permute-start(f32[8,128,128]{2,1,0:T(8,128)S(1)} %pad_maximum_fusion.2), channel_id=1, source_target_pairs={{0,4},{4,0},{8,12},{12,8},{16,20},{20,16},{24,28},{28,24},{1,5},{5... | collective-permute-start | bytes 1572872 | tf_op jit(solution)/shard_map/ppermute | solution.py:281
  65.4 12.0 %copy-start.45 = (f32[16,128,128]{2,1,0:T(8,128)S(1)}, f32[16,128,128]{2,1,0:T(8,128)}, u32[]{:S(2)}) copy-start(f32[16,128,128]{2,1,0:T(8,128)} %copy-done.44) | copy-start | bytes 3145732
  65.4 12.1 %copy-start.33 = (f32[16,4,128,128]{3,2,1,0:T(8,128)S(1)}, f32[16,4,128,128]{3,2,1,0:T(8,128)}, u32[]{:S(2)}) copy-start(f32[16,4,128,128]{3,2,1,0:T(8,128)} %copy-done.32) | copy-start | bytes 12582916
  77.2 20.6 %copy-start.9 = (bf16[16,128,1024]{2,1,0:T(8,128)(2,1)}, bf16[16,128,1024]{2,1,0:T(8,128)(2,1)S(1)}, u32[]{:S(2)}) copy-start(bf16[16,128,1024]{2,1,0:T(8,128)(2,1)S(1)} %get-tuple-element.120.q_ref.refs_4_) | copy-start | bytes 12582916
  88.7 12.5 %copy-start.4 = (f32[16,128,1024]{2,1,0:T(8,128)}, f32[16,128,1024]{2,1,0:T(8,128)S(1)}, u32[]{:S(2)}) copy-start(f32[16,128,1024]{2,1,0:T(8,128)S(1)} %get-tuple-element.127.refs_6_.attn_ref) | copy-start | bytes 25165828
  88.7 12.5 %copy-start.36 = (bf16[16,4,128,128]{3,2,1,0:T(8,128)(2,1)}, bf16[16,4,128,128]{3,2,1,0:T(8,128)(2,1)S(1)}, u32[]{:S(2)}) copy-start(bf16[16,4,128,128]{3,2,1,0:T(8,128)(2,1)S(1)} %get-tuple-element.131.held_ref) | copy-start | bytes 6291460
  88.7 5.0 %collective-permute-start.11 = (f32[2,1024]{1,0:T(2,128)S(1)}, f32[2,1024]{1,0:T(2,128)S(1)}, u32[]{:S(2)}, u32[]{:S(2)}) collective-permute-start(f32[2,1024]{1,0:T(2,128)S(1)} %get-tuple-element.126.refs_0_), channel_id=1, source_target_pairs={{0,3},{1,0},{2,1},{3,2},{4,7},{5,4},{6,5},{7,6},{8,11},{9,8},{10,9... | collective-permute-start | bytes 24584 | tf_op jit(solution)/shard_map/ppermute | solution.py:461
  92.4 4.5 %collective-permute-start.10 = (f32[2,1024]{1,0:T(2,128)S(1)}, f32[2,1024]{1,0:T(2,128)S(1)}, u32[]{:S(2)}, u32[]{:S(2)}) collective-permute-start(f32[2,1024]{1,0:T(2,128)S(1)} %get-tuple-element.126.refs_0_), channel_id=1, source_target_pairs={{0,2},{1,3},{2,0},{3,1},{4,6},{5,7},{6,4},{7,5},{8,10},{9,11},{10,... | collective-permute-start | bytes 24584 | tf_op jit(solution)/shard_map/ppermute | solution.py:461
  92.4 5.4 %collective-permute-start.9 = (f32[2,1024]{1,0:T(2,128)S(1)}, f32[2,1024]{1,0:T(2,128)S(1)}, u32[]{:S(2)}, u32[]{:S(2)}) collective-permute-start(f32[2,1024]{1,0:T(2,128)S(1)} %get-tuple-element.126.refs_0_), channel_id=1, source_target_pairs={{0,1},{1,2},{2,3},{3,0},{4,5},{5,6},{6,7},{7,4},{8,9},{9,10},{10,1... | collective-permute-start | bytes 24584 | tf_op jit(solution)/shard_map/ppermute | solution.py:461
  105.4 27.7 %collective-permute-start.12 = (f32[16,128,128]{2,1,0:T(8,128)S(1)}, f32[16,128,128]{2,1,0:T(8,128)}, u32[]{:S(2)}, u32[]{:S(2)}) collective-permute-start(f32[16,128,128]{2,1,0:T(8,128)S(1)} %get-tuple-element.128), channel_id=1, source_target_pairs={{0,4},{4,0},{8,12},{12,8},{16,20},{20,16},{24,28},{28,24},{1,5},{5... | collective-permute-start | bytes 3145736 | tf_op jit(solution)/shard_map/ppermute | solution.py:281
  136.0 24.9 %collective-permute-start.14 = (f32[4,128,128]{2,1,0:T(8,128)S(1)}, f32[4,128,128]{2,1,0:T(8,128)S(1)}, u32[]{:S(2)}, u32[]{:S(2)}) collective-permute-start(f32[4,128,128]{2,1,0:T(8,128)S(1)} %get-tuple-element.175), channel_id=1, source_target_pairs={{0,16},{4,20},{8,24},{12,28},{16,0},{20,4},{24,8},{28,12},{1,17},{... | collective-permute-start | bytes 786440 | tf_op jit(solution)/shard_map/ppermute | solution.py:281
  136.5 24.3 %collective-permute-start.13 = (f32[4,128,128]{2,1,0:T(8,128)S(1)}, f32[4,128,128]{2,1,0:T(8,128)S(1)}, u32[]{:S(2)}, u32[]{:S(2)}) collective-permute-start(f32[4,128,128]{2,1,0:T(8,128)S(1)} %get-tuple-element.176), channel_id=1, source_target_pairs={{0,8},{4,12},{8,0},{12,4},{16,24},{20,28},{24,16},{28,20},{1,9},{5... | collective-permute-start | bytes 786440 | tf_op jit(solution)/shard_map/ppermute | solution.py:281
  161.0 13.1 %collective-permute-start.15 = (f32[4,128,128]{2,1,0:T(8,128)S(1)}, f32[4,128,128]{2,1,0:T(8,128)S(1)}, u32[]{:S(2)}, u32[]{:S(2)}) collective-permute-start(f32[4,128,128]{2,1,0:T(8,128)S(1)} %get-tuple-element.174), channel_id=1, source_target_pairs={{0,16},{4,20},{8,24},{12,28},{16,0},{20,4},{24,8},{28,12},{1,17},{... | collective-permute-start | bytes 786440 | tf_op jit(solution)/shard_map/ppermute | solution.py:281
  162.6 11.5 %collective-permute-start.16 = (f32[4,128,128]{2,1,0:T(8,128)S(1)}, f32[4,128,128]{2,1,0:T(8,128)S(1)}, u32[]{:S(2)}, u32[]{:S(2)}) collective-permute-start(f32[4,128,128]{2,1,0:T(8,128)S(1)} %get-tuple-element.173), channel_id=1, source_target_pairs={{0,8},{4,12},{8,0},{12,4},{16,24},{20,28},{24,16},{28,20},{1,9},{5... | collective-permute-start | bytes 786440 | tf_op jit(solution)/shard_map/ppermute | solution.py:281
  174.2 10.5 %collective-permute-start.17 = (f32[8,128,128]{2,1,0:T(8,128)S(1)}, f32[8,128,128]{2,1,0:T(8,128)S(1)}, u32[]{:S(2)}, u32[]{:S(2)}) collective-permute-start(f32[8,128,128]{2,1,0:T(8,128)S(1)} %pad_maximum_fusion.3), channel_id=1, source_target_pairs={{0,4},{4,0},{8,12},{12,8},{16,20},{20,16},{24,28},{28,24},{1,5},{5... | collective-permute-start | bytes 1572872 | tf_op jit(solution)/shard_map/ppermute | solution.py:281
  (40 other events, 133.5 us)
